TPU v7x, 512 devices: a whole 4x8x8 slice. The times are simulated.
512 devices in a mesh: tile: 128 (over y, z, core), lev: 4 (over x).
Axes of the slice: x: 4, y: 8, z: 8, core: 2. Of those that a mesh axis runs over, the one named last changes fastest.
Arguments:
- field: float32 [8, 256, 4096], P('lev', 'tile'), may hold values from -6 to 6
- kappa_sq: float32 [8, 256, 4096], P('lev', 'tile'), may hold values from 0.25 to 4
- noise: float32 [3, 8, 256, 4096], P(None, 'lev', 'tile'), may hold values from -6 to 6
- block_owner: int32 [8, 8192, 1], P('lev', 'tile'), may hold values from 0 to 127; in each aligned block of 64 rows (0 to 63, 64 to 127, ..., all dimensions but the last counted through in order) at most 2 rows name the same one
- block_cell: int32 [8, 8192], P('lev', 'tile'), may hold values from 0 to 63
- live_count: int32 [8, 128], P('lev', 'tile'), may hold values from 16 to 64, as said below
- obs_weight: bfloat16 [8, 8192, 16, 128], P('lev', 'tile'), may hold values from -0.5 to 0.5
- obs_value: float32 [8, 8192, 16], P('lev', 'tile'), may hold values from -6 to 6
- obs_prec: float32 [8, 8192, 16], P('lev', 'tile'), may hold values from 1 to 32
Outputs:
- sample: float32 [8, 256, 4096], P('lev', 'tile')
Inputs may be any that keep to these rules, and one draw needn't show every extreme that they name: `block_owner`: among the blocks of one shard (aligned blocks of 64) and one level, at most 2 name the same owner tile. `live_count`: some shard has all its blocks of level 0 live.
All inputs are finite; a program needn't handle non-finite values.
Results may differ from a plain program's by a relative error of at most 0.00085.
Values may be sent and summed in bfloat16 or wider, within the bound.
A program may use at most 64 MiB of HBM per device.

v0:
```python
import jax
import jax.numpy as jnp
from jax import lax
from jax.sharding import PartitionSpec as P

STEPS = 3


step_size = 0.003


def with_halo(cells, sides, width):
    for axis, dim in sides:
        count = lax.axis_size(axis)
        ends = count - 1
        head = lax.slice_in_dim(cells, 0, width, axis=dim)
        tail = lax.slice_in_dim(cells, cells.shape[dim] - width, cells.shape[dim], axis=dim)
        cells = jnp.concatenate(
            [
                lax.ppermute(tail, axis, [(i, (i + 1) % count) for i in range(ends)]),
                cells,
                lax.ppermute(head, axis, [((i + 1) % count, i) for i in range(ends)]),
            ],
            axis=dim,
        )
    return cells


def stencil(padded, kappa_in):
    core = padded[1:-1, 1:-1]
    near = padded[:-2, 1:-1] + padded[2:, 1:-1] + padded[1:-1, :-2] + padded[1:-1, 2:]
    near = near + jnp.roll(core, 1, 2) + jnp.roll(core, -1, 2)
    return (kappa_in + 6.0) * core - near


def rim_pass(values, kappa_in):
    padded = with_halo(values, (("lev", 0), ("tile", 1)), 1)
    return stencil(padded, kappa_in)


def per_device(
    field, kappa_sq, noise, block_owner, block_cell, live_count, obs_weight, obs_value, obs_prec
):
    levels, row_count, columns = field.shape
    block_span = obs_weight.shape[3]
    blocks = block_cell.shape[1]
    tile_count = lax.axis_size("tile")
    slots_peer = max(2, 2 * blocks // tile_count)
    slot_total = tile_count * slots_peer
    seg_total = row_count * columns // block_span
    owners = block_owner[:, :, 0]
    onehot = (owners[:, :, None] == jnp.arange(tile_count, dtype=jnp.int32)[None, None, :]).astype(
        jnp.int32
    )
    earlier = jnp.cumsum(onehot, axis=1) - onehot
    rank_in = jnp.sum(earlier * onehot, axis=2)
    slot_of = owners * slots_peer + rank_in
    level_ids = jnp.arange(levels, dtype=jnp.int32)[:, None]
    addresses = jnp.full((levels, slot_total), -1, jnp.int32).at[level_ids, slot_of].set(block_cell)
    wanted = lax.all_to_all(addresses, "tile", split_axis=1, concat_axis=1, tiled=True)
    wanted_idx = jnp.where(wanted >= 0, wanted, 0)
    alive = (jnp.arange(blocks, dtype=jnp.int32)[None, :] < live_count).astype(jnp.float32)
    noise_scale = (2.0 * step_size) ** 0.5
    shard_weight = obs_weight.astype(jnp.float32)
    state = field
    for step_index in range(STEPS):
        segments = state.reshape(levels, seg_total, block_span)
        outgoing = segments[level_ids, wanted_idx]
        returned = lax.all_to_all(
            outgoing.astype(jnp.bfloat16), "tile", split_axis=1, concat_axis=1, tiled=True
        ).astype(outgoing.dtype)
        gathered = jnp.take_along_axis(returned, slot_of[:, :, None], axis=1)
        predicted = jnp.einsum(
            "lboc,lbc->lbo", shard_weight, gathered, precision=lax.Precision.HIGHEST
        )
        misfit = obs_prec * alive[:, :, None] * (predicted - obs_value)
        adjoint = jnp.einsum("lboc,lbo->lbc", shard_weight, misfit, precision=lax.Precision.HIGHEST)
        buffer = (
            jnp.zeros((levels, slot_total, block_span), jnp.float32)
            .at[level_ids, slot_of]
            .set(adjoint)
        )
        arrived = lax.all_to_all(
            buffer.astype(jnp.bfloat16), "tile", split_axis=1, concat_axis=1, tiled=True
        ).astype(buffer.dtype)
        flat = (
            jnp.zeros((levels, seg_total, block_span), jnp.float32)
            .at[level_ids, wanted_idx]
            .add(arrived)
        )
        gradient = rim_pass(rim_pass(state, kappa_sq), kappa_sq) + flat.reshape(
            levels, row_count, columns
        )
        state = state - step_size * gradient + noise_scale * noise[step_index]
    return state


def solution(mesh):
    placed = (
        P("lev", "tile", None),
        P("lev", "tile", None),
        P(None, "lev", "tile", None),
        P("lev", "tile", None),
        P("lev", "tile"),
        P("lev", "tile"),
        P("lev", "tile", None, None),
        P("lev", "tile", None),
        P("lev", "tile", None),
    )
    return jax.shard_map(
        per_device, mesh=mesh, in_specs=placed, out_specs=P("lev", "tile", None), check_vma=False
    )
```

profile of v0, /device:TPU:1, one launch (start us, length us, event | category | flops | bytes accessed | tf_op | source)
XLA Modules:
  0.0 323.9 jit_solution(3067310403198431402)
XLA Ops:
  1.9 6.9 %scatter_fusion = s32[2,256]{1,0:T(2,128)S(1)} fusion(s32[2,256]{1,0:T(2,128)S(1)} %broadcast_in_dim.13, s32[128]{0:T(128)S(1)} %reshape.124, s32[128]{0:T(128)S(1)} %reshape.126), kind=kCustom, calls=%fused_computation.6 | custom fusion | bytes 2560 | tf_op jit(solution)/shard_map/scatter | solution.py:59
  9.7 18.6 %all-to-all-start = ((s32[2,128,2]{2,0,1:T(2,128)}), s32[2,128,2]{2,0,1:T(2,128)S(1)}, u32[]{:S(2)}, u32[]{:S(2)}) async-start(s32[2,128,2]{2,0,1:T(2,128)} %copy.22), calls=%async_computation | async-start | bytes 262144 | tf_op jit(solution)/shard_map/all_to_all | solution.py:60
  28.3 3.1 collective-permute-start
  31.4 1.3 collective-permute-start.1
  33.8 6.7 %all-to-all-done = s32[2,128,2]{2,0,1:T(2,128)S(1)} async-done(((s32[2,128,2]{2,0,1:T(2,128)}), s32[2,128,2]{2,0,1:T(2,128)S(1)}, u32[]{:S(2)}, u32[]{:S(2)}) %all-to-all-start) | async-done | bytes 2080 | tf_op jit(solution)/shard_map/all_to_all | solution.py:60
  40.8 2.9 collective-permute-start.3
  43.7 2.6 collective-permute-start.2
  46.4 3.2 gather_fusion
  49.6 0.8 copy.24
  50.4 9.5 %all-to-all-start.1 = ((bf16[2,256,128]{2,0,1:T(2,128)(2,1)}), bf16[2,256,128]{2,0,1:T(2,128)(2,1)S(1)}, u32[]{:S(2)}, u32[]{:S(2)}) async-start(bf16[2,256,128]{2,0,1:T(2,128)(2,1)} %copy.24), calls=%async_computation.1 | async-start | bytes 262144 | tf_op jit(solution)/shard_map/all_to_all | solution.py:69
  60.2 1.3 collective-permute-start.5
  61.5 4.0 %collective-permute-start.4 = (f32[1,2,4096]{2,1,0:T(2,128)S(1)}, f32[1,2,4096]{2,1,0:T(2,128)S(1)}, u32[]{:S(2)}, u32[]{:S(2)}) collective-permute-start(f32[1,2,4096]{2,1,0:T(2,128)S(1)} %get-tuple-element.44), channel_id=1, source_target_pairs={{0,1},{1,2},{2,3},{4,5},{5,6},{6,7},{8,9},{9,10},{10,11},{12,13},{... | collective-permute-start | bytes 98312 | tf_op jit(solution)/shard_map/ppermute | solution.py:20
  65.6 0.9 collective-permute-done.4
  66.6 5.4 %all-to-all-done.1 = bf16[2,256,128]{2,0,1:T(2,128)(2,1)S(1)} async-done(((bf16[2,256,128]{2,0,1:T(2,128)(2,1)}), bf16[2,256,128]{2,0,1:T(2,128)(2,1)S(1)}, u32[]{:S(2)}, u32[]{:S(2)}) %all-to-all-start.1) | async-done | bytes 131104 | tf_op jit(solution)/shard_map/all_to_all | solution.py:69
  72.0 1.2 gather_fusion.3
  73.4 0.9 fusion.76
  75.7 6.8 %scatter_fusion.1 = f32[2,256,128]{2,1,0:T(8,128)S(1)} fusion(f32[2,256,128]{2,1,0:T(8,128)S(1)} %broadcast.94.clone, s32[128]{0:T(128)S(1)} %reshape.124, f32[128,128]{1,0:T(8,128)S(1)} %bitcast.115), kind=kCustom, calls=%fused_computation.7 | custom fusion | bytes 197632 | tf_op jit(solution)/shard_map/scatter | solution.py:81
  82.5 0.8 copy.26
  83.3 9.5 %all-to-all-start.2 = ((bf16[2,256,128]{2,0,1:T(2,128)(2,1)}), bf16[2,256,128]{2,0,1:T(2,128)(2,1)S(1)}, u32[]{:S(2)}, u32[]{:S(2)}) async-start(bf16[2,256,128]{2,0,1:T(2,128)(2,1)} %copy.26), calls=%async_computation.2 | async-start | bytes 262144 | tf_op jit(solution)/shard_map/all_to_all | solution.py:83
  92.9 2.8 collective-permute-start.7
  95.7 2.8 collective-permute-start.6
  98.5 6.5 %all-to-all-done.2 = bf16[2,256,128]{2,0,1:T(2,128)(2,1)S(1)} async-done(((bf16[2,256,128]{2,0,1:T(2,128)(2,1)}), bf16[2,256,128]{2,0,1:T(2,128)(2,1)S(1)}, u32[]{:S(2)}, u32[]{:S(2)}) %all-to-all-start.2) | async-done | bytes 131104 | tf_op jit(solution)/shard_map/all_to_all | solution.py:83
  105.1 25.3 %scatter_fusion.2 = f32[2,64,128]{2,1,0:T(8,128)S(1)} fusion(f32[2,64,128]{2,1,0:T(8,128)S(1)} %broadcast.88.clone, s32[512]{0:T(512)S(1)} %bitcast.102, f32[512,128]{1,0:T(8,128)S(1)} %bitcast_convert_fusion.2), kind=kCustom, calls=%fused_computation.8 | custom fusion | flops 65536 | bytes 790528 | tf_op jit(solution)/shard_map/scatter-add | solution.py:89
  130.7 1.3 collective-permute-start.9
  132.0 4.6 %collective-permute-start.8 = (f32[1,2,4096]{2,1,0:T(2,128)S(1)}, f32[1,2,4096]{2,1,0:T(2,128)S(1)}, u32[]{:S(2)}, u32[]{:S(2)}) collective-permute-start(f32[1,2,4096]{2,1,0:T(2,128)S(1)} %get-tuple-element.42), channel_id=1, source_target_pairs={{0,1},{1,2},{2,3},{4,5},{5,6},{6,7},{8,9},{9,10},{10,11},{12,13},{... | collective-permute-start | bytes 98312 | tf_op jit(solution)/shard_map/ppermute | solution.py:20
  136.8 0.9 collective-permute-done.8
  137.9 3.8 %collective-permute-start.11 = (f32[4,1,4096]{2,1,0:T(1,128)S(1)}, f32[4,1,4096]{2,1,0:T(1,128)S(1)}, u32[]{:S(2)}, u32[]{:S(2)}) collective-permute-start(f32[4,1,4096]{2,1,0:T(1,128)S(1)} %get-tuple-element.15), channel_id=1, source_target_pairs={{4,0},{8,4},{12,8},{16,12},{20,16},{24,20},{28,24},{32,28},{36,32}... | collective-permute-start | bytes 196616 | tf_op jit(solution)/shard_map/ppermute | solution.py:22
  141.7 2.1 collective-permute-start.10
  143.9 3.2 gather_fusion.1
  147.1 0.8 copy.28
  147.9 8.3 %all-to-all-start.3 = ((bf16[2,256,128]{2,0,1:T(2,128)(2,1)}), bf16[2,256,128]{2,0,1:T(2,128)(2,1)S(1)}, u32[]{:S(2)}, u32[]{:S(2)}) async-start(bf16[2,256,128]{2,0,1:T(2,128)(2,1)} %copy.28), calls=%async_computation.3 | async-start | bytes 262144 | tf_op jit(solution)/shard_map/all_to_all | solution.py:69
  156.7 1.3 collective-permute-start.13
  158.0 4.6 %collective-permute-start.12 = (f32[1,2,4096]{2,1,0:T(2,128)S(1)}, f32[1,2,4096]{2,1,0:T(2,128)S(1)}, u32[]{:S(2)}, u32[]{:S(2)}) collective-permute-start(f32[1,2,4096]{2,1,0:T(2,128)S(1)} %get-tuple-element.32), channel_id=1, source_target_pairs={{0,1},{1,2},{2,3},{4,5},{5,6},{6,7},{8,9},{9,10},{10,11},{12,13},{... | collective-permute-start | bytes 98312 | tf_op jit(solution)/shard_map/ppermute | solution.py:20
  162.6 0.9 collective-permute-done.12
  163.6 4.8 %all-to-all-done.3 = bf16[2,256,128]{2,0,1:T(2,128)(2,1)S(1)} async-done(((bf16[2,256,128]{2,0,1:T(2,128)(2,1)}), bf16[2,256,128]{2,0,1:T(2,128)(2,1)S(1)}, u32[]{:S(2)}, u32[]{:S(2)}) %all-to-all-start.3) | async-done | bytes 131104 | tf_op jit(solution)/shard_map/all_to_all | solution.py:69
  168.5 1.2 gather_fusion.4
  169.8 0.9 fusion.78
  171.5 6.8 %scatter_fusion.3 = f32[2,256,128]{2,1,0:T(8,128)S(1)} fusion(f32[2,256,128]{2,1,0:T(8,128)S(1)} %broadcast.94.clone.1, s32[128]{0:T(128)S(1)} %reshape.124, f32[128,128]{1,0:T(8,128)S(1)} %bitcast.116), kind=kCustom, calls=%fused_computation.9 | custom fusion | bytes 197632 | tf_op jit(solution)/shard_map/scatter | solution.py:81
  179.1 9.8 %all-to-all-start.4 = ((bf16[2,256,128]{2,0,1:T(2,128)(2,1)}), bf16[2,256,128]{2,0,1:T(2,128)(2,1)S(1)}, u32[]{:S(2)}, u32[]{:S(2)}) async-start(bf16[2,256,128]{2,0,1:T(2,128)(2,1)} %copy.30), calls=%async_computation.4 | async-start | bytes 262144 | tf_op jit(solution)/shard_map/all_to_all | solution.py:83
  189.0 2.8 collective-permute-start.15
  191.8 3.0 collective-permute-start.14
  194.8 6.3 %all-to-all-done.4 = bf16[2,256,128]{2,0,1:T(2,128)(2,1)S(1)} async-done(((bf16[2,256,128]{2,0,1:T(2,128)(2,1)}), bf16[2,256,128]{2,0,1:T(2,128)(2,1)S(1)}, u32[]{:S(2)}, u32[]{:S(2)}) %all-to-all-start.4) | async-done | bytes 131104 | tf_op jit(solution)/shard_map/all_to_all | solution.py:83
  201.1 25.3 %scatter_fusion.4 = f32[2,64,128]{2,1,0:T(8,128)S(1)} fusion(f32[2,64,128]{2,1,0:T(8,128)S(1)} %broadcast.88.clone.1, s32[512]{0:T(512)S(1)} %bitcast.103, f32[512,128]{1,0:T(8,128)S(1)} %bitcast_convert_fusion.1), kind=kCustom, calls=%fused_computation.10 | custom fusion | flops 65536 | bytes 790528 | tf_op jit(solution)/shard_map/scatter-add | solution.py:89
  226.8 1.3 collective-permute-start.17
  228.1 4.6 %collective-permute-start.16 = (f32[1,2,4096]{2,1,0:T(2,128)S(1)}, f32[1,2,4096]{2,1,0:T(2,128)S(1)}, u32[]{:S(2)}, u32[]{:S(2)}) collective-permute-start(f32[1,2,4096]{2,1,0:T(2,128)S(1)} %get-tuple-element.30), channel_id=1, source_target_pairs={{0,1},{1,2},{2,3},{4,5},{5,6},{6,7},{8,9},{9,10},{10,11},{12,13},{... | collective-permute-start | bytes 98312 | tf_op jit(solution)/shard_map/ppermute | solution.py:20
  232.9 0.9 collective-permute-done.16
  233.9 3.8 %collective-permute-start.19 = (f32[4,1,4096]{2,1,0:T(1,128)S(1)}, f32[4,1,4096]{2,1,0:T(1,128)S(1)}, u32[]{:S(2)}, u32[]{:S(2)}) collective-permute-start(f32[4,1,4096]{2,1,0:T(1,128)S(1)} %get-tuple-element.11), channel_id=1, source_target_pairs={{4,0},{8,4},{12,8},{16,12},{20,16},{24,20},{28,24},{32,28},{36,32}... | collective-permute-start | bytes 196616 | tf_op jit(solution)/shard_map/ppermute | solution.py:22
  237.7 2.1 collective-permute-start.18
  240.0 3.2 gather_fusion.2
  243.2 0.8 copy.32
  244.0 8.6 %all-to-all-start.5 = ((bf16[2,256,128]{2,0,1:T(2,128)(2,1)}), bf16[2,256,128]{2,0,1:T(2,128)(2,1)S(1)}, u32[]{:S(2)}, u32[]{:S(2)}) async-start(bf16[2,256,128]{2,0,1:T(2,128)(2,1)} %copy.32), calls=%async_computation.5 | async-start | bytes 262144 | tf_op jit(solution)/shard_map/all_to_all | solution.py:69
  253.0 1.3 collective-permute-start.21
  254.3 4.7 %collective-permute-start.20 = (f32[1,2,4096]{2,1,0:T(2,128)S(1)}, f32[1,2,4096]{2,1,0:T(2,128)S(1)}, u32[]{:S(2)}, u32[]{:S(2)}) collective-permute-start(f32[1,2,4096]{2,1,0:T(2,128)S(1)} %get-tuple-element.20), channel_id=1, source_target_pairs={{0,1},{1,2},{2,3},{4,5},{5,6},{6,7},{8,9},{9,10},{10,11},{12,13},{... | collective-permute-start | bytes 98312 | tf_op jit(solution)/shard_map/ppermute | solution.py:20
  259.1 0.9 collective-permute-done.20
  260.1 4.7 %all-to-all-done.5 = bf16[2,256,128]{2,0,1:T(2,128)(2,1)S(1)} async-done(((bf16[2,256,128]{2,0,1:T(2,128)(2,1)}), bf16[2,256,128]{2,0,1:T(2,128)(2,1)S(1)}, u32[]{:S(2)}, u32[]{:S(2)}) %all-to-all-start.5) | async-done | bytes 131104 | tf_op jit(solution)/shard_map/all_to_all | solution.py:69
  264.8 1.2 gather_fusion.5
  266.1 0.9 fusion.80
  267.8 6.8 %scatter_fusion.5 = f32[2,256,128]{2,1,0:T(8,128)S(1)} fusion(f32[2,256,128]{2,1,0:T(8,128)S(1)} %broadcast.94, s32[128]{0:T(128)S(1)} %reshape.124, f32[128,128]{1,0:T(8,128)S(1)} %bitcast.114), kind=kCustom, calls=%fused_computation.11 | custom fusion | bytes 197632 | tf_op jit(solution)/shard_map/scatter | solution.py:81
  275.4 9.9 %all-to-all-start.6 = ((bf16[2,256,128]{2,0,1:T(2,128)(2,1)}), bf16[2,256,128]{2,0,1:T(2,128)(2,1)S(1)}, u32[]{:S(2)}, u32[]{:S(2)}) async-start(bf16[2,256,128]{2,0,1:T(2,128)(2,1)} %copy.34), calls=%async_computation.6 | async-start | bytes 262144 | tf_op jit(solution)/shard_map/all_to_all | solution.py:83
  285.5 2.8 collective-permute-start.23
  288.3 2.8 collective-permute-start.22
  291.0 6.5 %all-to-all-done.6 = bf16[2,256,128]{2,0,1:T(2,128)(2,1)S(1)} async-done(((bf16[2,256,128]{2,0,1:T(2,128)(2,1)}), bf16[2,256,128]{2,0,1:T(2,128)(2,1)S(1)}, u32[]{:S(2)}, u32[]{:S(2)}) %all-to-all-start.6) | async-done | bytes 131104 | tf_op jit(solution)/shard_map/all_to_all | solution.py:83
  297.6 25.3 %scatter_fusion.6 = f32[2,64,128]{2,1,0:T(8,128)S(1)} fusion(f32[2,64,128]{2,1,0:T(8,128)S(1)} %broadcast.88, s32[512]{0:T(512)S(1)} %bitcast.104, f32[512,128]{1,0:T(8,128)S(1)} %bitcast_convert_fusion), kind=kCustom, calls=%fused_computation.12 | custom fusion | flops 65536 | bytes 790528 | tf_op jit(solution)/shard_map/scatter-add | solution.py:89
  323.0 0.9 bitcast_add_fusion
  (132 shorter events, 12.5 us)
Async XLA Ops:
  0.0 73.4 %copy-start = (bf16[2,64,16,128]{3,2,1,0:T(8,128)(2,1)S(1)}, bf16[2,64,16,128]{3,2,1,0:T(8,128)(2,1)}, u32[]{:S(2)}) copy-start(bf16[2,64,16,128]{3,2,1,0:T(8,128)(2,1)} %param.17) | copy-start | bytes 1572868
  0.0 0.7 copy-start.6
  1.1 0.7 copy-start.7
  9.7 18.6 %copy-start.1 = (f32[2,2,4096]{2,1,0:T(2,128)S(1)}, f32[2,2,4096]{2,1,0:T(2,128)}, u32[]{:S(2)}) copy-start(f32[2,2,4096]{2,1,0:T(2,128)} %param.11) | copy-start | bytes 196612
  9.7 30.8 %all-to-all-start = ((s32[2,128,2]{2,0,1:T(2,128)}), s32[2,128,2]{2,0,1:T(2,128)S(1)}, u32[]{:S(2)}, u32[]{:S(2)}) async-start(s32[2,128,2]{2,0,1:T(2,128)} %copy.22), calls=%async_computation | async-start | bytes 262144 | tf_op jit(solution)/shard_map/all_to_all | solution.py:60
  28.3 12.3 %collective-permute-start = (f32[1,2,4096]{2,1,0:T(2,128)S(1)}, f32[1,2,4096]{2,1,0:T(2,128)S(1)}, u32[]{:S(2)}, u32[]{:S(2)}) collective-permute-start(f32[1,2,4096]{2,1,0:T(2,128)S(1)} %get-tuple-element.55), channel_id=1, source_target_pairs={{0,1},{1,2},{2,3},{4,5},{5,6},{6,7},{8,9},{9,10},{10,11},{12,13},{... | collective-permute-start | bytes 98312 | tf_op jit(solution)/shard_map/ppermute | solution.py:20
  31.4 9.2 %collective-permute-start.1 = (f32[1,2,4096]{2,1,0:T(2,128)S(1)}, f32[1,2,4096]{2,1,0:T(2,128)S(1)}, u32[]{:S(2)}, u32[]{:S(2)}) collective-permute-start(f32[1,2,4096]{2,1,0:T(2,128)S(1)} %get-tuple-element.54), channel_id=1, source_target_pairs={{1,0},{2,1},{3,2},{5,4},{6,5},{7,6},{9,8},{10,9},{11,10},{13,12},{... | collective-permute-start | bytes 98312 | tf_op jit(solution)/shard_map/ppermute | solution.py:22
  32.9 0.7 copy-start.8
  40.8 19.1 %collective-permute-start.3 = (f32[4,1,4096]{2,1,0:T(1,128)S(1)}, f32[4,1,4096]{2,1,0:T(1,128)S(1)}, u32[]{:S(2)}, u32[]{:S(2)}) collective-permute-start(f32[4,1,4096]{2,1,0:T(1,128)S(1)} %get-tuple-element.19), channel_id=1, source_target_pairs={{4,0},{8,4},{12,8},{16,12},{20,16},{24,20},{28,24},{32,28},{36,32}... | collective-permute-start | bytes 196616 | tf_op jit(solution)/shard_map/ppermute | solution.py:22
  43.7 16.1 %collective-permute-start.2 = (f32[4,1,4096]{2,1,0:T(1,128)S(1)}, f32[4,1,4096]{2,1,0:T(1,128)S(1)}, u32[]{:S(2)}, u32[]{:S(2)}) collective-permute-start(f32[4,1,4096]{2,1,0:T(1,128)S(1)} %get-tuple-element.18), channel_id=1, source_target_pairs={{0,4},{4,8},{8,12},{12,16},{16,20},{20,24},{24,28},{28,32},{32,36}... | collective-permute-start | bytes 196616 | tf_op jit(solution)/shard_map/ppermute | solution.py:20
  50.4 9.5 %copy-start.2 = (f32[2,2,4096]{2,1,0:T(2,128)S(1)}, f32[2,2,4096]{2,1,0:T(2,128)}, u32[]{:S(2)}) copy-start(f32[2,2,4096]{2,1,0:T(2,128)} %param.12) | copy-start | bytes 196612
  50.4 21.7 %all-to-all-start.1 = ((bf16[2,256,128]{2,0,1:T(2,128)(2,1)}), bf16[2,256,128]{2,0,1:T(2,128)(2,1)S(1)}, u32[]{:S(2)}, u32[]{:S(2)}) async-start(bf16[2,256,128]{2,0,1:T(2,128)(2,1)} %copy.24), calls=%async_computation.1 | async-start | bytes 262144 | tf_op jit(solution)/shard_map/all_to_all | solution.py:69
  60.2 5.4 %collective-permute-start.5 = (f32[1,2,4096]{2,1,0:T(2,128)S(1)}, f32[1,2,4096]{2,1,0:T(2,128)S(1)}, u32[]{:S(2)}, u32[]{:S(2)}) collective-permute-start(f32[1,2,4096]{2,1,0:T(2,128)S(1)} %get-tuple-element.45), channel_id=1, source_target_pairs={{1,0},{2,1},{3,2},{5,4},{6,5},{7,6},{9,8},{10,9},{11,10},{13,12},{... | collective-permute-start | bytes 98312 | tf_op jit(solution)/shard_map/ppermute | solution.py:22
  61.5 5.0 %collective-permute-start.4 = (f32[1,2,4096]{2,1,0:T(2,128)S(1)}, f32[1,2,4096]{2,1,0:T(2,128)S(1)}, u32[]{:S(2)}, u32[]{:S(2)}) collective-permute-start(f32[1,2,4096]{2,1,0:T(2,128)S(1)} %get-tuple-element.44), channel_id=1, source_target_pairs={{0,1},{1,2},{2,3},{4,5},{5,6},{6,7},{8,9},{9,10},{10,11},{12,13},{... | collective-permute-start | bytes 98312 | tf_op jit(solution)/shard_map/ppermute | solution.py:20
  74.3 0.7 copy-start.4
  74.3 0.7 copy-start.5
  83.3 21.7 %all-to-all-start.2 = ((bf16[2,256,128]{2,0,1:T(2,128)(2,1)}), bf16[2,256,128]{2,0,1:T(2,128)(2,1)S(1)}, u32[]{:S(2)}, u32[]{:S(2)}) async-start(bf16[2,256,128]{2,0,1:T(2,128)(2,1)} %copy.26), calls=%async_computation.2 | async-start | bytes 262144 | tf_op jit(solution)/shard_map/all_to_all | solution.py:83
  92.9 37.5 %collective-permute-start.7 = (f32[4,1,4096]{2,1,0:T(1,128)S(1)}, f32[4,1,4096]{2,1,0:T(1,128)S(1)}, u32[]{:S(2)}, u32[]{:S(2)}) collective-permute-start(f32[4,1,4096]{2,1,0:T(1,128)S(1)} %get-tuple-element.17), channel_id=1, source_target_pairs={{4,0},{8,4},{12,8},{16,12},{20,16},{24,20},{28,24},{32,28},{36,32}... | collective-permute-start | bytes 196616 | tf_op jit(solution)/shard_map/ppermute | solution.py:22
  95.7 34.7 %collective-permute-start.6 = (f32[4,1,4096]{2,1,0:T(1,128)S(1)}, f32[4,1,4096]{2,1,0:T(1,128)S(1)}, u32[]{:S(2)}, u32[]{:S(2)}) collective-permute-start(f32[4,1,4096]{2,1,0:T(1,128)S(1)} %get-tuple-element.16), channel_id=1, source_target_pairs={{0,4},{4,8},{8,12},{12,16},{16,20},{20,24},{24,28},{28,32},{32,36}... | collective-permute-start | bytes 196616 | tf_op jit(solution)/shard_map/ppermute | solution.py:20
  105.1 25.4 %copy-start.3 = (f32[3,2,2,4096]{3,2,1,0:T(2,128)S(1)}, f32[3,2,2,4096]{3,2,1,0:T(2,128)}, u32[]{:S(2)}) copy-start(f32[3,2,2,4096]{3,2,1,0:T(2,128)} %param.13) | copy-start | bytes 589828
  130.7 6.1 %collective-permute-start.9 = (f32[1,2,4096]{2,1,0:T(2,128)S(1)}, f32[1,2,4096]{2,1,0:T(2,128)S(1)}, u32[]{:S(2)}, u32[]{:S(2)}) collective-permute-start(f32[1,2,4096]{2,1,0:T(2,128)S(1)} %get-tuple-element.43), channel_id=1, source_target_pairs={{1,0},{2,1},{3,2},{5,4},{6,5},{7,6},{9,8},{10,9},{11,10},{13,12},{... | collective-permute-start | bytes 98312 | tf_op jit(solution)/shard_map/ppermute | solution.py:22
  132.0 5.7 %collective-permute-start.8 = (f32[1,2,4096]{2,1,0:T(2,128)S(1)}, f32[1,2,4096]{2,1,0:T(2,128)S(1)}, u32[]{:S(2)}, u32[]{:S(2)}) collective-permute-start(f32[1,2,4096]{2,1,0:T(2,128)S(1)} %get-tuple-element.42), channel_id=1, source_target_pairs={{0,1},{1,2},{2,3},{4,5},{5,6},{6,7},{8,9},{9,10},{10,11},{12,13},{... | collective-permute-start | bytes 98312 | tf_op jit(solution)/shard_map/ppermute | solution.py:20
  137.9 18.4 %collective-permute-start.11 = (f32[4,1,4096]{2,1,0:T(1,128)S(1)}, f32[4,1,4096]{2,1,0:T(1,128)S(1)}, u32[]{:S(2)}, u32[]{:S(2)}) collective-permute-start(f32[4,1,4096]{2,1,0:T(1,128)S(1)} %get-tuple-element.15), channel_id=1, source_target_pairs={{4,0},{8,4},{12,8},{16,12},{20,16},{24,20},{28,24},{32,28},{36,32}... | collective-permute-start | bytes 196616 | tf_op jit(solution)/shard_map/ppermute | solution.py:22
  141.7 14.6 %collective-permute-start.10 = (f32[4,1,4096]{2,1,0:T(1,128)S(1)}, f32[4,1,4096]{2,1,0:T(1,128)S(1)}, u32[]{:S(2)}, u32[]{:S(2)}) collective-permute-start(f32[4,1,4096]{2,1,0:T(1,128)S(1)} %get-tuple-element.14), channel_id=1, source_target_pairs={{0,4},{4,8},{8,12},{12,16},{16,20},{20,24},{24,28},{28,32},{32,36}... | collective-permute-start | bytes 196616 | tf_op jit(solution)/shard_map/ppermute | solution.py:20
  147.9 20.5 %all-to-all-start.3 = ((bf16[2,256,128]{2,0,1:T(2,128)(2,1)}), bf16[2,256,128]{2,0,1:T(2,128)(2,1)S(1)}, u32[]{:S(2)}, u32[]{:S(2)}) async-start(bf16[2,256,128]{2,0,1:T(2,128)(2,1)} %copy.28), calls=%async_computation.3 | async-start | bytes 262144 | tf_op jit(solution)/shard_map/all_to_all | solution.py:69
  156.7 6.0 %collective-permute-start.13 = (f32[1,2,4096]{2,1,0:T(2,128)S(1)}, f32[1,2,4096]{2,1,0:T(2,128)S(1)}, u32[]{:S(2)}, u32[]{:S(2)}) collective-permute-start(f32[1,2,4096]{2,1,0:T(2,128)S(1)} %get-tuple-element.33), channel_id=1, source_target_pairs={{1,0},{2,1},{3,2},{5,4},{6,5},{7,6},{9,8},{10,9},{11,10},{13,12},{... | collective-permute-start | bytes 98312 | tf_op jit(solution)/shard_map/ppermute | solution.py:22
  158.0 5.6 %collective-permute-start.12 = (f32[1,2,4096]{2,1,0:T(2,128)S(1)}, f32[1,2,4096]{2,1,0:T(2,128)S(1)}, u32[]{:S(2)}, u32[]{:S(2)}) collective-permute-start(f32[1,2,4096]{2,1,0:T(2,128)S(1)} %get-tuple-element.32), channel_id=1, source_target_pairs={{0,1},{1,2},{2,3},{4,5},{5,6},{6,7},{8,9},{9,10},{10,11},{12,13},{... | collective-permute-start | bytes 98312 | tf_op jit(solution)/shard_map/ppermute | solution.py:20
  179.1 22.0 %all-to-all-start.4 = ((bf16[2,256,128]{2,0,1:T(2,128)(2,1)}), bf16[2,256,128]{2,0,1:T(2,128)(2,1)S(1)}, u32[]{:S(2)}, u32[]{:S(2)}) async-start(bf16[2,256,128]{2,0,1:T(2,128)(2,1)} %copy.30), calls=%async_computation.4 | async-start | bytes 262144 | tf_op jit(solution)/shard_map/all_to_all | solution.py:83
  189.0 37.5 %collective-permute-start.15 = (f32[4,1,4096]{2,1,0:T(1,128)S(1)}, f32[4,1,4096]{2,1,0:T(1,128)S(1)}, u32[]{:S(2)}, u32[]{:S(2)}) collective-permute-start(f32[4,1,4096]{2,1,0:T(1,128)S(1)} %get-tuple-element.13), channel_id=1, source_target_pairs={{4,0},{8,4},{12,8},{16,12},{20,16},{24,20},{28,24},{32,28},{36,32}... | collective-permute-start | bytes 196616 | tf_op jit(solution)/shard_map/ppermute | solution.py:22
  191.8 34.7 %collective-permute-start.14 = (f32[4,1,4096]{2,1,0:T(1,128)S(1)}, f32[4,1,4096]{2,1,0:T(1,128)S(1)}, u32[]{:S(2)}, u32[]{:S(2)}) collective-permute-start(f32[4,1,4096]{2,1,0:T(1,128)S(1)} %get-tuple-element.12), channel_id=1, source_target_pairs={{0,4},{4,8},{8,12},{12,16},{16,20},{20,24},{24,28},{28,32},{32,36}... | collective-permute-start | bytes 196616 | tf_op jit(solution)/shard_map/ppermute | solution.py:20
  226.8 6.1 %collective-permute-start.17 = (f32[1,2,4096]{2,1,0:T(2,128)S(1)}, f32[1,2,4096]{2,1,0:T(2,128)S(1)}, u32[]{:S(2)}, u32[]{:S(2)}) collective-permute-start(f32[1,2,4096]{2,1,0:T(2,128)S(1)} %get-tuple-element.31), channel_id=1, source_target_pairs={{1,0},{2,1},{3,2},{5,4},{6,5},{7,6},{9,8},{10,9},{11,10},{13,12},{... | collective-permute-start | bytes 98312 | tf_op jit(solution)/shard_map/ppermute | solution.py:22
  228.1 5.6 %collective-permute-start.16 = (f32[1,2,4096]{2,1,0:T(2,128)S(1)}, f32[1,2,4096]{2,1,0:T(2,128)S(1)}, u32[]{:S(2)}, u32[]{:S(2)}) collective-permute-start(f32[1,2,4096]{2,1,0:T(2,128)S(1)} %get-tuple-element.30), channel_id=1, source_target_pairs={{0,1},{1,2},{2,3},{4,5},{5,6},{6,7},{8,9},{9,10},{10,11},{12,13},{... | collective-permute-start | bytes 98312 | tf_op jit(solution)/shard_map/ppermute | solution.py:20
  233.9 18.7 %collective-permute-start.19 = (f32[4,1,4096]{2,1,0:T(1,128)S(1)}, f32[4,1,4096]{2,1,0:T(1,128)S(1)}, u32[]{:S(2)}, u32[]{:S(2)}) collective-permute-start(f32[4,1,4096]{2,1,0:T(1,128)S(1)} %get-tuple-element.11), channel_id=1, source_target_pairs={{4,0},{8,4},{12,8},{16,12},{20,16},{24,20},{28,24},{32,28},{36,32}... | collective-permute-start | bytes 196616 | tf_op jit(solution)/shard_map/ppermute | solution.py:22
  237.7 14.9 %collective-permute-start.18 = (f32[4,1,4096]{2,1,0:T(1,128)S(1)}, f32[4,1,4096]{2,1,0:T(1,128)S(1)}, u32[]{:S(2)}, u32[]{:S(2)}) collective-permute-start(f32[4,1,4096]{2,1,0:T(1,128)S(1)} %get-tuple-element.10), channel_id=1, source_target_pairs={{0,4},{4,8},{8,12},{12,16},{16,20},{20,24},{24,28},{28,32},{32,36}... | collective-permute-start | bytes 196616 | tf_op jit(solution)/shard_map/ppermute | solution.py:20
  244.0 20.8 %all-to-all-start.5 = ((bf16[2,256,128]{2,0,1:T(2,128)(2,1)}), bf16[2,256,128]{2,0,1:T(2,128)(2,1)S(1)}, u32[]{:S(2)}, u32[]{:S(2)}) async-start(bf16[2,256,128]{2,0,1:T(2,128)(2,1)} %copy.32), calls=%async_computation.5 | async-start | bytes 262144 | tf_op jit(solution)/shard_map/all_to_all | solution.py:69
  253.0 6.1 %collective-permute-start.21 = (f32[1,2,4096]{2,1,0:T(2,128)S(1)}, f32[1,2,4096]{2,1,0:T(2,128)S(1)}, u32[]{:S(2)}, u32[]{:S(2)}) collective-permute-start(f32[1,2,4096]{2,1,0:T(2,128)S(1)} %get-tuple-element.21), channel_id=1, source_target_pairs={{1,0},{2,1},{3,2},{5,4},{6,5},{7,6},{9,8},{10,9},{11,10},{13,12},{... | collective-permute-start | bytes 98312 | tf_op jit(solution)/shard_map/ppermute | solution.py:22
  254.3 5.7 %collective-permute-start.20 = (f32[1,2,4096]{2,1,0:T(2,128)S(1)}, f32[1,2,4096]{2,1,0:T(2,128)S(1)}, u32[]{:S(2)}, u32[]{:S(2)}) collective-permute-start(f32[1,2,4096]{2,1,0:T(2,128)S(1)} %get-tuple-element.20), channel_id=1, source_target_pairs={{0,1},{1,2},{2,3},{4,5},{5,6},{6,7},{8,9},{9,10},{10,11},{12,13},{... | collective-permute-start | bytes 98312 | tf_op jit(solution)/shard_map/ppermute | solution.py:20
  275.4 22.1 %all-to-all-start.6 = ((bf16[2,256,128]{2,0,1:T(2,128)(2,1)}), bf16[2,256,128]{2,0,1:T(2,128)(2,1)S(1)}, u32[]{:S(2)}, u32[]{:S(2)}) async-start(bf16[2,256,128]{2,0,1:T(2,128)(2,1)} %copy.34), calls=%async_computation.6 | async-start | bytes 262144 | tf_op jit(solution)/shard_map/all_to_all | solution.py:83
  285.5 37.5 %collective-permute-start.23 = (f32[4,1,4096]{2,1,0:T(1,128)S(1)}, f32[4,1,4096]{2,1,0:T(1,128)S(1)}, u32[]{:S(2)}, u32[]{:S(2)}) collective-permute-start(f32[4,1,4096]{2,1,0:T(1,128)S(1)} %get-tuple-element.9), channel_id=1, source_target_pairs={{4,0},{8,4},{12,8},{16,12},{20,16},{24,20},{28,24},{32,28},{36,32}... | collective-permute-start | bytes 196616 | tf_op jit(solution)/shard_map/ppermute | solution.py:22
  288.3 34.7 %collective-permute-start.22 = (f32[4,1,4096]{2,1,0:T(1,128)S(1)}, f32[4,1,4096]{2,1,0:T(1,128)S(1)}, u32[]{:S(2)}, u32[]{:S(2)}) collective-permute-start(f32[4,1,4096]{2,1,0:T(1,128)S(1)} %get-tuple-element.8), channel_id=1, source_target_pairs={{0,4},{4,8},{8,12},{12,16},{16,20},{20,24},{24,28},{28,32},{32,36}... | collective-permute-start | bytes 196616 | tf_op jit(solution)/shard_map/ppermute | solution.py:20
where the time goes:
time: 327 us; the launch traced here: 324 us
  starting transfers between devices  142 us (43%)
  other arithmetic  79.3 us (24%)
  local copies, waits for them, and re-layouts  51.8 us (16%)
  waiting for transfers between devices  45.4 us (14%)
  matrix products  4.47 us (1%)
    scatter-add x3, other arithmetic, per_device(): flat = jnp.zeros((levels, seg_total, block_span), jnp.float32).at[level_i...  75.9 us
    ppermute x12, starting transfers between devices, with_halo(): lax.ppermute(tail, axis, [(i, (i + 1) % count) for i in range(ends)])  41.1 us
    all_to_all x3, starting transfers between devices, per_device(): lax.all_to_all(buffer.astype(jnp.bfloat16), 'tile', split_axis=1, concat_...  29.2 us
    ppermute x12, starting transfers between devices, with_halo(): lax.ppermute(head, axis, [((i + 1) % count, i) for i in range(ends)])  26.7 us
    all_to_all x3, starting transfers between devices, per_device(): lax.all_to_all(outgoing.astype(jnp.bfloat16), 'tile', split_axis=1, conca...  26.4 us
    scatter x3, local copies, waits for them, and re-layouts, per_device(): buffer = jnp.zeros((levels, slot_total, block_span), jnp.float32).at[leve...  20.3 us
    all_to_all x3, waiting for transfers between devices, per_device(): lax.all_to_all(buffer.astype(jnp.bfloat16), 'tile', split_axis=1, concat_...  19.3 us
    all_to_all x1, starting transfers between devices, per_device(): lax.all_to_all(addresses, 'tile', split_axis=1, concat_axis=1, tiled=True)  18.6 us
  transfers between devices with their start and end apart: 31, of which 12 were waited for; matrix products, arithmetic and copies ran while one was open for 28% of the time, Pallas kernels for 0%

commit v1 on v0

v1 whole, which is shorter than its diff:
```python
import jax
import jax.numpy as jnp
from jax import lax
from jax.sharding import PartitionSpec as P
from jax.experimental import pallas as pl
from jax.experimental.pallas import tpu as pltpu

STEPS = 3
STEP = 0.003
NOISE_SCALE = (2.0 * STEP) ** 0.5
MESH = pl.DeviceIdType.MESH
BF = jnp.bfloat16
F32 = jnp.float32
RING = 8


def ring_distance(d):
    return min(d, RING - d)


def hops(delta):
    return ring_distance(delta[0]) + ring_distance(delta[1])


PEERS = sorted(
    [(a, b, c) for a in range(RING) for b in range(RING) for c in range(2) if (a, b, c) != (0, 0, 0)],
    key=lambda d: (-hops(d), (d[0] + 3 * d[1]) % 4, d),
)
SELF = len(PEERS)
GROUPS = SELF + 1
SLOTS = 4
ROWS = GROUPS * SLOTS


def dot(a, b, dims=((1,), (0,)), **kw):
    return lax.dot_general(a, b, (dims, ((), ())), preferred_element_type=F32, **kw)


def iota(shape, dim):
    return lax.broadcasted_iota(jnp.int32, shape, dim)


def kernel_body(
    slot_ref, field_ref, kappa_ref, noise_ref, owner_ref, cell_ref, live_ref, weight_ref, value_ref, prec_ref,
    out_ref,
    trip_out, trip_in, halo_x, halo_k, x_buf, k_buf, pick_ref, pick_t_ref, gain_ref, offset_ref, weight_t_ref,
    trip_send, trip_recv, halo_send, halo_recv,
):
    me = lax.axis_index("tile")
    lev = lax.axis_index("lev")
    tiles = 2 * RING * RING
    y, z, c = me // (2 * RING), (me // 2) % RING, me % 2
    at_y = [((y + d) % RING) * (2 * RING) for d in range(RING)]
    at_z = [((z + d) % RING) * 2 for d in range(RING)]
    at_c = [c, 1 - c]

    def peer(delta):
        return at_y[delta[0]] + at_z[delta[1]] + at_c[delta[2]]

    above, below = (lev + 1) % 4, (lev + 3) % 4
    north, south = (me + 1) % tiles, (me + tiles - 1) % tiles

    greet = pltpu.get_barrier_semaphore()
    for delta in PEERS:
        pl.semaphore_signal(greet, inc=1, device_id=(peer(delta), lev), device_id_type=MESH)
    beside = [(me, above), (me, below), (north, above), (north, below), (south, above), (south, below)]
    for device in beside:
        pl.semaphore_signal(greet, inc=1, device_id=device, device_id_type=MESH)

    for l in range(2):
        for r in range(2):
            x_buf[0, 2 * l + r] = field_ref[l, r : r + 1, :].reshape(32, 128)
            k_buf[2 * l + r] = kappa_ref[l, r : r + 1, :].reshape(32, 128)

    owner = owner_ref[...].reshape(128, 1)
    level_of = iota((128, 1), 0) // 64
    slot_peer = slot_ref[0:1, :]
    slot_y, slot_z, slot_c = slot_ref[1:2, :], slot_ref[2:3, :], slot_ref[3:4, :]
    slot_peer = ((y + slot_y) % RING) * (2 * RING) + ((z + slot_z) % RING) * 2 + (c + slot_c) % 2
    slot_j = iota((1, ROWS), 1) % SLOTS
    row_i, col_i = iota((128, 128), 0), iota((128, 128), 1)
    named = (owner == col_i).astype(F32)
    before = ((col_i < row_i) & (col_i // 64 == row_i // 64)).astype(BF)
    rank = jnp.sum(dot(before, named.astype(BF)) * named, axis=1, keepdims=True)
    block_j = 2 * level_of + rank.astype(jnp.int32)
    pick = ((owner == slot_peer) & (block_j == slot_j)).astype(F32)
    pick_ref[...] = pick.astype(BF)
    pick_t = pick.T.astype(BF)
    pick_t_ref[...] = pick_t
    cells = jnp.concatenate([cell_ref[0:1, :], cell_ref[1:2, :]], axis=1)
    cell_t = ((row_i // 64 == col_i // 64) & (row_i % 64 == cells)).astype(BF)
    request = dot(pick_t, cell_t, ((1,), (1,))).astype(BF).reshape(GROUPS, SLOTS, 128)
    trip_out[0] = request
    trip_in[0, SELF] = request[SELF]

    alive = jnp.concatenate(
        [(iota((64, 1), 0) < live_ref[l : l + 1, :]).astype(F32) for l in range(2)], axis=0
    )
    spread = (iota((16, 256), 1) % 16 == iota((16, 256), 0)).astype(F32)
    own = (iota((128, 256), 1) // 16 == iota((128, 256), 0) % 16).astype(F32)
    gain = prec_ref[...].reshape(128, 16) * alive
    offset = gain * value_ref[...].reshape(128, 16)
    gain_ref[...] = dot(gain, spread, precision=lax.Precision.HIGHEST) * own
    offset_ref[...] = dot(offset, spread, precision=lax.Precision.HIGHEST) * own
    for p in range(8):
        w = weight_ref[p // 4, 16 * (p % 4) : 16 * (p % 4) + 16].reshape(256, 128)
        weight_t_ref[p] = w.T

    pl.semaphore_wait(greet, len(PEERS) + len(beside))

    def trip_copy(t, i, delta):
        if t % 2:
            delta = ((RING - delta[0]) % RING, (RING - delta[1]) % RING, delta[2])
        return pltpu.make_async_remote_copy(
            trip_out.at[t, i], trip_in.at[t, i], trip_send.at[t], trip_recv.at[t],
            device_id=(peer(delta), lev), device_id_type=MESH,
        )

    def trip_all(t):
        return pltpu.make_async_remote_copy(
            trip_out.at[t, pl.ds(0, SELF)], trip_in.at[t, pl.ds(0, SELF)], trip_send.at[t], trip_recv.at[t],
            device_id=(north, lev), device_id_type=MESH,
        )

    def start_trip(t):
        for i, delta in enumerate(PEERS):
            trip_copy(t, i, delta).start()

    def halo_copy(src, dst, s, device):
        return pltpu.make_async_remote_copy(
            src, dst, halo_send.at[s], halo_recv.at[s], device_id=device, device_id_type=MESH
        )

    def start_halo(k):
        x = x_buf.at[k]
        into = halo_x.at[k]
        halo_copy(x, into.at[pl.ds(0, 4)], k, (me, above)).start()
        halo_copy(x, into.at[pl.ds(4, 4)], k, (me, below)).start()
        halo_copy(x, into.at[pl.ds(8, 4)], k, (north, lev)).start()
        halo_copy(x, into.at[pl.ds(12, 4)], k, (south, lev)).start()
        halo_copy(x.at[3], into.at[16], k, (north, above)).start()
        halo_copy(x.at[2], into.at[17], k, (south, above)).start()
        halo_copy(x.at[1], into.at[18], k, (north, below)).start()
        halo_copy(x.at[0], into.at[19], k, (south, below)).start()

    def halo_all(k):
        return halo_copy(halo_x.at[k], halo_x.at[k], k, (north, lev))

    def start_kappa():
        halo_copy(k_buf.at[pl.ds(2, 2)], halo_k.at[pl.ds(0, 2)], STEPS, (me, above)).start()
        halo_copy(k_buf.at[pl.ds(0, 2)], halo_k.at[pl.ds(2, 2)], STEPS, (me, below)).start()
        for l in range(2):
            halo_copy(k_buf.at[2 * l + 1], halo_k.at[4 + l], STEPS, (north, lev)).start()
            halo_copy(k_buf.at[2 * l], halo_k.at[6 + l], STEPS, (south, lev)).start()

    def kappa_all():
        return halo_copy(halo_k, halo_k, STEPS, (north, lev))

    start_trip(0)
    start_halo(0)
    start_kappa()

    lane = iota((32, 128), 1)
    has = {
        (-1, 0): lev > 0, (1, 0): lev < 3, (0, -1): me > 0, (0, 1): me < tiles - 1,
    }

    def stencil(v, kap, near):
        left = pltpu.roll(v, 1, 1)
        left = jnp.where(lane == 0, pltpu.roll(left, 1, 0), left)
        right = pltpu.roll(v, 127, 1)
        right = jnp.where(lane == 127, pltpu.roll(right, 31, 0), right)
        return (kap + 6.0) * v - (near + left + right)

    def prior(k):
        halo_all(k).wait_recv()
        if k == 0:
            kappa_all().wait_recv()
        v, kap = {}, {}
        for l in range(2):
            for r in range(2):
                v[l, r] = x_buf[k, 2 * l + r]
                kap[l, r] = k_buf[2 * l + r]
                v[l - 2, r] = halo_x[k, 2 * l + r]
                v[l + 2, r] = halo_x[k, 4 + 2 * l + r]
                v[l, r - 2] = halo_x[k, 8 + 2 * l + r]
                v[l, r + 2] = halo_x[k, 12 + 2 * l + r]
        v[-1, -1], v[-1, 2], v[2, -1], v[2, 2] = (halo_x[k, 16 + q] for q in range(4))
        for q in range(2):
            kap[-1, q], kap[2, q] = halo_k[q], halo_k[2 + q]
            kap[q, -1], kap[q, 2] = halo_k[4 + q], halo_k[6 + q]

        def inside(l, r):
            conds = []
            if l < 0:
                conds.append(has[-1, 0])
            if l > 1:
                conds.append(has[1, 0])
            if r < 0:
                conds.append(has[0, -1])
            if r > 1:
                conds.append(has[0, 1])
            return conds

        def masked(p, l, r):
            for cond in inside(l, r):
                p = jnp.where(cond, p, 0.0)
            return p

        v = {at: masked(p, *at) for at, p in v.items()}
        once = {}
        for l, r in list(kap):
            near = v[l - 1, r] + v[l + 1, r] + v[l, r - 1] + v[l, r + 1]
            once[l, r] = masked(stencil(v[l, r], kap[l, r], near), l, r)
        planes = []
        for l in range(2):
            for r in range(2):
                near = once[l - 1, r] + once[l + 1, r] + once[l, r - 1] + once[l, r + 1]
                twice = stencil(once[l, r], kap[l, r], near)
                noise = noise_ref[k, l, r : r + 1, :].reshape(32, 128)
                planes.append(v[l, r] - STEP * twice + NOISE_SCALE * noise)
        return planes

    wanted = None
    for k in range(STEPS):
        x = x_buf[k].reshape(128, 128).astype(BF)
        if k == 0:
            trip_all(0).wait_recv()
            wanted = trip_in[0].reshape(ROWS, 128)
        send = dot(wanted, x).astype(BF).reshape(GROUPS, SLOTS, 128)
        trip_out[1 + 2 * k] = send
        trip_in[1 + 2 * k, SELF] = send[SELF]
        start_trip(1 + 2 * k)
        if k > 0:
            start_halo(k)
        planes = prior(k)
        trip_all(1 + 2 * k).wait_recv()
        cells_in = dot(pick_ref[...], trip_in[1 + 2 * k].reshape(ROWS, 128)).astype(BF)
        parts = []
        for p in range(8):
            seen = dot(cells_in[16 * p : 16 * p + 16], weight_t_ref[p])
            misfit = gain_ref[16 * p : 16 * p + 16] * seen - offset_ref[16 * p : 16 * p + 16]
            w = weight_ref[p // 4, 16 * (p % 4) : 16 * (p % 4) + 16].reshape(256, 128)
            parts.append(dot(misfit.astype(BF), w).astype(BF))
        adjoint = jnp.concatenate(parts, axis=0)
        send = dot(pick_t_ref[...], adjoint).astype(BF).reshape(GROUPS, SLOTS, 128)
        trip_out[2 + 2 * k] = send
        trip_in[2 + 2 * k, SELF] = send[SELF]
        start_trip(2 + 2 * k)
        trip_all(2 + 2 * k).wait_recv()
        total = dot(wanted, trip_in[2 + 2 * k].reshape(ROWS, 128), ((0,), (0,)))
        for l in range(2):
            for r in range(2):
                q = 2 * l + r
                new = planes[q] - STEP * total[32 * q : 32 * q + 32]
                if k + 1 < STEPS:
                    x_buf[k + 1, q] = new
                else:
                    out_ref[l, r : r + 1, :] = new.reshape(1, 4096)

    for t in range(1 + 2 * STEPS):
        trip_all(t).wait_send()
    for k in range(STEPS):
        halo_all(k).wait_send()
    kappa_all().wait_send()


def per_device(slots, *arrays):
    vmem = pl.BlockSpec(memory_space=pltpu.VMEM)
    trips = 1 + 2 * STEPS
    return pl.pallas_call(
        kernel_body,
        out_shape=jax.ShapeDtypeStruct((2, 2, 4096), F32),
        in_specs=[vmem] * 10,
        out_specs=vmem,
        scratch_shapes=[
            pltpu.VMEM((trips, GROUPS, SLOTS, 128), BF),
            pltpu.VMEM((trips, GROUPS, SLOTS, 128), BF),
            pltpu.VMEM((STEPS, 20, 32, 128), F32),
            pltpu.VMEM((8, 32, 128), F32),
            pltpu.VMEM((STEPS, 4, 32, 128), F32),
            pltpu.VMEM((4, 32, 128), F32),
            pltpu.VMEM((128, ROWS), BF),
            pltpu.VMEM((ROWS, 128), BF),
            pltpu.VMEM((128, 256), F32),
            pltpu.VMEM((128, 256), F32),
            pltpu.VMEM((8, 128, 256), BF),
            pltpu.SemaphoreType.DMA((trips,)),
            pltpu.SemaphoreType.DMA((trips,)),
            pltpu.SemaphoreType.DMA((STEPS + 1,)),
            pltpu.SemaphoreType.DMA((STEPS + 1,)),
        ],
        compiler_params=pltpu.CompilerParams(
            collective_id=0, has_side_effects=True, vmem_limit_bytes=48 << 20
        ),
        cost_estimate=pl.CostEstimate(flops=200_000_000, bytes_accessed=1_000_000, transcendentals=0),
    )(slots, *arrays)


def slot_table():
    deltas = PEERS + [(0, 0, 0)]
    table = [[0] * ROWS for _ in range(8)]
    for i, delta in enumerate(deltas):
        for j in range(SLOTS):
            for q in range(3):
                table[1 + q][SLOTS * i + j] = delta[q]
    return jnp.array(table, jnp.int32)


def solution(mesh):
    placed = (
        P("lev", "tile", None),
        P("lev", "tile", None),
        P(None, "lev", "tile", None),
        P("lev", "tile", None),
        P("lev", "tile"),
        P("lev", "tile"),
        P("lev", "tile", None, None),
        P("lev", "tile", None),
        P("lev", "tile", None),
    )
    run = jax.shard_map(
        per_device, mesh=mesh, in_specs=(P(None, None),) + placed, out_specs=P("lev", "tile", None), check_vma=False
    )

    def sample(*arrays):
        return run(slot_table(), *arrays)

    return sample
```

time: 327 us -> 79.1 us (0.24)
  starting transfers between devices: 142 us -> 0 us
  other arithmetic: 79.3 us -> 0 us
  Pallas kernels: 0 us -> 72.8 us
  local copies, waits for them, and re-layouts: 51.8 us -> 5.87 us
  waiting for transfers between devices: 45.4 us -> 0 us
  matrix products: 4.47 us -> 0 us
    scatter-add x3 -> x0, other arithmetic: 75.9 us -> none  [per_device(): flat = jnp.zeros((levels, seg_total, block_span), jnp.float32).at[level_i...]
    all_to_all x7 -> x0, starting transfers between devices: 74.2 us -> none  [the longest x3 29.2 us: per_device(): lax.all_to_all(buffer.astype(jnp.bfloat16), 'tile', split_axis=1, concat_...]
    pallas_call x0 -> x1, Pallas kernels: none -> 72.8 us  [per_device(): pl.pallas_call(kernel_body, out_shape=jax.ShapeDtypeStruct((2, 2, 4096),...]
    ppermute x24 -> x0, starting transfers between devices: 67.8 us -> none  [the longest x12 41.1 us: with_halo(): lax.ppermute(tail, axis, [(i, (i + 1) % count) for i in range(ends)])]
    all_to_all x7 -> x0, waiting for transfers between devices: 40.9 us -> none  [the longest x3 19.3 us: per_device(): lax.all_to_all(buffer.astype(jnp.bfloat16), 'tile', split_axis=1, concat_...]
    scatter x4 -> x0, local copies, waits for them, and re-layouts: 27.2 us -> none  [the longest x3 20.3 us: per_device(): buffer = jnp.zeros((levels, slot_total, block_span), jnp.float32).at[leve...]
    gather x7 -> x0, local copies, waits for them, and re-layouts: 13.3 us -> none  [the longest x3 9.54 us: per_device(): outgoing = segments[level_ids, wanted_idx]]
    convert_element_type x6 -> x0, local copies, waits for them, and re-layouts: 4.68 us -> none  [the longest x3 2.34 us: per_device(): outgoing.astype(jnp.bfloat16)]
  transfers between devices with their start and end apart: 31 -> 0, of which waited for: 12 -> 0; matrix products, arithmetic and copies ran while one was open for 28% -> 0% of each run, Pallas kernels for 0% -> 0%
where the time goes in v1:
time: 79.1 us; the launch traced here: 78.8 us
  Pallas kernels  72.8 us (92%)
  local copies, waits for them, and re-layouts  5.87 us (7%)
    pallas_call x1, Pallas kernels, per_device(): pl.pallas_call(kernel_body, out_shape=jax.ShapeDtypeStruct((2, 2, 4096),...  72.8 us
    unnamed x19, local copies, waits for them, and re-layouts  5.87 us

profile of v1, /device:TPU:1, one launch (start us, length us, event | category | flops | bytes accessed | tf_op | source)
XLA Modules:
  0.0 78.8 jit_solution(2658008797655933189)
XLA Ops:
  0.0 0.0 copy-start.6
  0.0 0.0 copy-start.1
  0.0 0.8 copy.12.live_ref
  0.8 0.0 copy-done.6
  0.8 0.1 copy.11.owner_ref
  0.9 0.8 %copy.13.value_ref = f32[2,64,16]{2,1,0:T(8,128)S(1)} copy(f32[2,64,16]{1,2,0:T(8,128)} %param.17) | data formatting | bytes 16384 | tf_op args[7]
  1.7 0.0 copy-start.4
  1.7 0.0 copy-start.5
  1.7 0.8 %copy.14.prec_ref = f32[2,64,16]{2,1,0:T(8,128)S(1)} copy(f32[2,64,16]{1,2,0:T(8,128)} %param.18) | data formatting | bytes 16384 | tf_op args[8]
  2.5 0.0 copy-done.1
  2.5 0.0 copy-done.4
  2.5 0.0 copy-done.5
  2.6 0.0 copy-start
  2.6 1.0 %copy-done = bf16[2,64,16,128]{3,2,1,0:T(8,128)(2,1)S(1)} copy-done((bf16[2,64,16,128]{3,2,1,0:T(8,128)(2,1)S(1)}, bf16[2,64,16,128]{3,2,1,0:T(8,128)(2,1)}, u32[]{:S(2)}) %copy-start) | copy-done | bytes 524312
  3.6 0.0 copy-start.2
  3.6 0.8 %copy-done.2 = f32[2,2,4096]{2,1,0:T(2,128)S(1)} copy-done((f32[2,2,4096]{2,1,0:T(2,128)S(1)}, f32[2,2,4096]{2,1,0:T(2,128)}, u32[]{:S(2)}) %copy-start.2) | copy-done | bytes 65560
  4.4 0.0 copy-start.3
  4.4 0.8 %copy-done.3 = f32[2,2,4096]{2,1,0:T(2,128)S(1)} copy-done((f32[2,2,4096]{2,1,0:T(2,128)S(1)}, f32[2,2,4096]{2,1,0:T(2,128)}, u32[]{:S(2)}) %copy-start.3) | copy-done | bytes 65560
  5.3 72.8 %shard_map.100 = f32[2,2,4096]{2,1,0:T(2,128)S(1)} custom-call(s32[8,512]{1,0:T(8,128)S(1)} %copy-done.4, f32[2,2,4096]{2,1,0:T(2,128)S(1)} %copy-done.2, f32[2,2,4096]{2,1,0:T(2,128)S(1)} %copy-done.3, f32[3,2,2,4096]{3,2,1,0:T(2,128)S(1)} %copy-done.1, s32[2,64,1]{2,1,0:T(8,128)S(1)} %copy.11.owner_ref, s32[2,64]{1,0:T(2,128)S(1)} %copy-done.5, ...), custom_call_target="tpu_custom_call" | custom-call | flops 200000000 | bytes 1000000 | tf_op jit(solution)/shard_map/pallas_call | solution.py:271
  78.1 0.6 copy.16
Async XLA Ops:
  0.0 0.8 copy-start.6
  0.0 2.5 %copy-start.1 = (f32[3,2,2,4096]{3,2,1,0:T(2,128)S(1)}, f32[3,2,2,4096]{3,2,1,0:T(2,128)}, u32[]{:S(2)}) copy-start(f32[3,2,2,4096]{3,2,1,0:T(2,128)} %noise_ref.1) | copy-start | bytes 589828
  1.7 0.8 %copy-start.4 = (s32[8,512]{1,0:T(8,128)S(1)}, s32[8,512]{1,0:T(8,128)}, u32[]{:S(2)}) copy-start(s32[8,512]{1,0:T(8,128)} %constant.2.clone.slot_ref) | copy-start | bytes 49156
  1.7 0.8 %copy-start.5 = (s32[2,64]{1,0:T(2,128)S(1)}, s32[2,64]{1,0:T(2,128)}, u32[]{:S(2)}) copy-start(s32[2,64]{1,0:T(2,128)} %cell_ref.1) | copy-start | bytes 1540
  2.6 1.0 %copy-start = (bf16[2,64,16,128]{3,2,1,0:T(8,128)(2,1)S(1)}, bf16[2,64,16,128]{3,2,1,0:T(8,128)(2,1)}, u32[]{:S(2)}) copy-start(bf16[2,64,16,128]{3,2,1,0:T(8,128)(2,1)} %weight_ref.1) | copy-start | bytes 1572868
  3.6 0.8 %copy-start.2 = (f32[2,2,4096]{2,1,0:T(2,128)S(1)}, f32[2,2,4096]{2,1,0:T(2,128)}, u32[]{:S(2)}) copy-start(f32[2,2,4096]{2,1,0:T(2,128)} %field_ref.1) | copy-start | bytes 196612
  4.4 0.8 %copy-start.3 = (f32[2,2,4096]{2,1,0:T(2,128)S(1)}, f32[2,2,4096]{2,1,0:T(2,128)}, u32[]{:S(2)}) copy-start(f32[2,2,4096]{2,1,0:T(2,128)} %kappa_ref.1) | copy-start | bytes 196612

commit v2 on v1

--- a/solution.py
+++ b/solution.py
@@ -30,6 +30,26 @@
 GROUPS = SELF + 1
 SLOTS = 4
 ROWS = GROUPS * SLOTS
+FAR = 32
+
+OUTWARD = (4, 3, 5, 2, 6, 1, 7)
+LINE_ROWS = 2 * RING
+
+
+def along(l, e):
+    return (e, 0, 0) if l == 0 else (0, e, 0)
+
+
+def across(l, q):
+    return (0, q // 2, q % 2) if l == 0 else (q // 2, 0, q % 2)
+
+
+def negative(delta):
+    return ((RING - delta[0]) % RING, (RING - delta[1]) % RING, delta[2])
+
+
+ACROSS = [2 * d + c for d in OUTWARD for c in (1, 0)] + [1]
+GREETED = sorted({across(l, q) for l in range(2) for q in ACROSS})
 
 
 def dot(a, b, dims=((1,), (0,)), **kw):
@@ -41,10 +61,12 @@
 
 
 def kernel_body(
+    slot_hbm, field_hbm, kappa_hbm, noise_hbm, owner_hbm, cell_hbm, live_hbm, weight_hbm, value_hbm, prec_hbm,
+    out_ref,
     slot_ref, field_ref, kappa_ref, noise_ref, owner_ref, cell_ref, live_ref, weight_ref, value_ref, prec_ref,
-    out_ref,
     trip_out, trip_in, halo_x, halo_k, x_buf, k_buf, pick_ref, pick_t_ref, gain_ref, offset_ref, weight_t_ref,
-    trip_send, trip_recv, halo_send, halo_recv,
+    wanted_t_ref, seed_out, seed_in, ask_out, ask_in, answer_out, answer_in, pick_line_ref,
+    trip_send, trip_recv, halo_send, halo_recv, load_sem, line_send, line_recv,
 ):
     me = lax.axis_index("tile")
     lev = lax.axis_index("lev")
@@ -61,70 +83,75 @@
     north, south = (me + 1) % tiles, (me + tiles - 1) % tiles
 
     greet = pltpu.get_barrier_semaphore()
-    for delta in PEERS:
+    for delta in GREETED:
         pl.semaphore_signal(greet, inc=1, device_id=(peer(delta), lev), device_id_type=MESH)
-    beside = [(me, above), (me, below), (north, above), (north, below), (south, above), (south, below)]
+    beside = [(north, lev), (south, lev), (me, above), (me, below), (north, above), (north, below), (south, above), (south, below)]
     for device in beside:
         pl.semaphore_signal(greet, inc=1, device_id=device, device_id_type=MESH)
 
+    loads = [
+        pltpu.make_async_copy(src, dst, load_sem.at[i])
+        for i, (src, dst) in enumerate(
+            [
+                (owner_hbm, owner_ref), (cell_hbm, cell_ref), (slot_hbm, slot_ref), (field_hbm, field_ref),
+                (kappa_hbm, kappa_ref), (live_hbm, live_ref), (prec_hbm, prec_ref), (value_hbm, value_ref),
+                (weight_hbm, weight_ref), (noise_hbm, noise_ref),
+            ]
+        )
+    ]
+    for load in loads:
+        load.start()
+    for load in loads[:5]:
+        load.wait()
     for l in range(2):
         for r in range(2):
             x_buf[0, 2 * l + r] = field_ref[l, r : r + 1, :].reshape(32, 128)
             k_buf[2 * l + r] = kappa_ref[l, r : r + 1, :].reshape(32, 128)
 
-    owner = owner_ref[...].reshape(128, 1)
+    owner_row = jnp.concatenate([owner_ref[0], owner_ref[1]], axis=1).astype(F32)
+    owner = jnp.broadcast_to(owner_row, (128, 128)).T.astype(jnp.int32)[:, 0:1]
     level_of = iota((128, 1), 0) // 64
-    slot_peer = slot_ref[0:1, :]
-    slot_y, slot_z, slot_c = slot_ref[1:2, :], slot_ref[2:3, :], slot_ref[3:4, :]
-    slot_peer = ((y + slot_y) % RING) * (2 * RING) + ((z + slot_z) % RING) * 2 + (c + slot_c) % 2
-    slot_j = iota((1, ROWS), 1) % SLOTS
     row_i, col_i = iota((128, 128), 0), iota((128, 128), 1)
     named = (owner == col_i).astype(F32)
     before = ((col_i < row_i) & (col_i // 64 == row_i // 64)).astype(BF)
-    rank = jnp.sum(dot(before, named.astype(BF)) * named, axis=1, keepdims=True)
-    block_j = 2 * level_of + rank.astype(jnp.int32)
-    pick = ((owner == slot_peer) & (block_j == slot_j)).astype(F32)
-    pick_ref[...] = pick.astype(BF)
-    pick_t = pick.T.astype(BF)
-    pick_t_ref[...] = pick_t
-    cells = jnp.concatenate([cell_ref[0:1, :], cell_ref[1:2, :]], axis=1)
-    cell_t = ((row_i // 64 == col_i // 64) & (row_i % 64 == cells)).astype(BF)
-    request = dot(pick_t, cell_t, ((1,), (1,))).astype(BF).reshape(GROUPS, SLOTS, 128)
-    trip_out[0] = request
-    trip_in[0, SELF] = request[SELF]
-
-    alive = jnp.concatenate(
-        [(iota((64, 1), 0) < live_ref[l : l + 1, :]).astype(F32) for l in range(2)], axis=0
-    )
-    spread = (iota((16, 256), 1) % 16 == iota((16, 256), 0)).astype(F32)
-    own = (iota((128, 256), 1) // 16 == iota((128, 256), 0) % 16).astype(F32)
-    gain = prec_ref[...].reshape(128, 16) * alive
-    offset = gain * value_ref[...].reshape(128, 16)
-    gain_ref[...] = dot(gain, spread, precision=lax.Precision.HIGHEST) * own
-    offset_ref[...] = dot(offset, spread, precision=lax.Precision.HIGHEST) * own
-    for p in range(8):
-        w = weight_ref[p // 4, 16 * (p % 4) : 16 * (p % 4) + 16].reshape(256, 128)
-        weight_t_ref[p] = w.T
-
-    pl.semaphore_wait(greet, len(PEERS) + len(beside))
-
-    def trip_copy(t, i, delta):
-        if t % 2:
-            delta = ((RING - delta[0]) % RING, (RING - delta[1]) % RING, delta[2])
+    rank = jnp.sum(dot(before, named.astype(BF)) * named, axis=1, keepdims=True).astype(jnp.int32)
+    n = iota((1, 256), 1)
+    for l in range(2):
+        x_flat = jnp.concatenate([x_buf[0, 2 * l], x_buf[0, 2 * l + 1]], axis=0).astype(BF)
+        seed_out[l] = x_flat
+        seed_in[l, 0] = x_flat
+        e, d = (n // 2) % RING, n // 32
+        dy, dz = (e, d) if l == 0 else (d, e)
+        line_peer = ((y + dy) % RING) * (2 * RING) + ((z + dz) % RING) * 2 + (c + (n // 16) % 2) % 2
+        mine = slice(64 * l, 64 * l + 64)
+        pick_line = ((owner[mine] == line_peer) & (rank[mine] == n % 2)).astype(F32)
+        pick_line_ref[l] = pick_line.astype(BF)
+        cell_line = (row_i[:, :64] % 64 == cell_ref[l : l + 1, :]).astype(F32).T.astype(BF)
+        ask = dot(pick_line.T.astype(BF), cell_line).astype(BF).reshape(2 * RING, LINE_ROWS, 128)
+        ask_out[l] = ask
+        ask_in[l, 0] = ask[0]
+
+    pl.semaphore_wait(greet, len(GREETED) + len(beside))
+
+    def line_copy(src, dst, what, l, delta):
         return pltpu.make_async_remote_copy(
-            trip_out.at[t, i], trip_in.at[t, i], trip_send.at[t], trip_recv.at[t],
+            src, dst, line_send.at[what, l], line_recv.at[what, l],
             device_id=(peer(delta), lev), device_id_type=MESH,
         )
 
-    def trip_all(t):
-        return pltpu.make_async_remote_copy(
-            trip_out.at[t, pl.ds(0, SELF)], trip_in.at[t, pl.ds(0, SELF)], trip_send.at[t], trip_recv.at[t],
-            device_id=(north, lev), device_id_type=MESH,
-        )
-
-    def start_trip(t):
-        for i, delta in enumerate(PEERS):
-            trip_copy(t, i, delta).start()
+    rest = pl.ds(1, RING - 1)
+    others = pl.ds(1, 2 * RING - 1)
+
+    def line_all(what, l):
+        ref = seed_in.at[l, rest] if what == 0 else (ask_in if what == 1 else answer_in).at[l, others]
+        return line_copy(ref, ref, what, l, (0, 0, 1))
+
+    for e in OUTWARD:
+        for l in range(2):
+            line_copy(seed_out.at[l], seed_in.at[l, RING - e], 0, l, along(l, e)).start()
+    for q in ACROSS:
+        for l in range(2):
+            line_copy(ask_out.at[l, q], ask_in.at[l, q], 1, l, across(l, q)).start()
 
     def halo_copy(src, dst, s, device):
         return pltpu.make_async_remote_copy(
@@ -156,9 +183,68 @@
     def kappa_all():
         return halo_copy(halo_k, halo_k, STEPS, (north, lev))
 
-    start_trip(0)
     start_halo(0)
     start_kappa()
+
+    slot_peer = slot_ref[0:1, :]
+    slot_y, slot_z, slot_c = slot_ref[1:2, :], slot_ref[2:3, :], slot_ref[3:4, :]
+    slot_peer = ((y + slot_y) % RING) * (2 * RING) + ((z + slot_z) % RING) * 2 + (c + slot_c) % 2
+    slot_j = iota((1, ROWS), 1) % SLOTS
+    block_j = 2 * level_of + rank
+    pick = ((owner == slot_peer) & (block_j == slot_j)).astype(F32)
+    pick_ref[...] = pick.astype(BF)
+    pick_t = pick.T.astype(BF)
+    pick_t_ref[...] = pick_t
+    cells = jnp.concatenate([cell_ref[0:1, :], cell_ref[1:2, :]], axis=1)
+    cell_t = ((row_i // 64 == col_i // 64) & (row_i % 64 == cells)).astype(BF)
+    cell = cell_t.T
+
+    for load in loads[5:]:
+        load.wait()
+    block_row = iota((1, 128), 1)
+    lives = jnp.where(block_row < 64, live_ref[0:1, 0:1], live_ref[0:1, 1:2])
+    alive = (block_row % 64 < lives).astype(F32)
+    spread = (iota((16, 256), 1) % 16 == iota((16, 256), 0)).astype(F32)
+    own = (iota((128, 256), 1) // 16 == iota((128, 256), 0) % 16).astype(F32)
+    gain = jnp.concatenate([prec_ref[0], prec_ref[1]], axis=1) * alive
+    offset = gain * jnp.concatenate([value_ref[0], value_ref[1]], axis=1)
+    gain_ref[...] = dot(gain.T, spread, precision=lax.Precision.HIGHEST) * own
+    offset_ref[...] = dot(offset.T, spread, precision=lax.Precision.HIGHEST) * own
+    for p in range(8):
+        w = weight_ref[p // 4, 16 * (p % 4) : 16 * (p % 4) + 16].reshape(256, 128)
+        weight_t_ref[p] = w.T
+
+    def trip_copy(t, i, delta):
+        if t in (2, 4):
+            delta = negative(delta)
+        part = int(i >= FAR)
+        return pltpu.make_async_remote_copy(
+            trip_out.at[t, i], trip_in.at[t, i], trip_send.at[t, part], trip_recv.at[t, part],
+            device_id=(peer(delta), lev), device_id_type=MESH,
+        )
+
+    def trip_part(t, part):
+        span = pl.ds(0, FAR) if part == 0 else pl.ds(FAR, SELF - FAR)
+        return pltpu.make_async_remote_copy(
+            trip_out.at[t, span], trip_in.at[t, span], trip_send.at[t, part], trip_recv.at[t, part],
+            device_id=(north, lev), device_id_type=MESH,
+        )
+
+    def start_trip(t, lhs, rhs):
+        for part, (lo, hi) in enumerate(((0, FAR), (FAR, GROUPS))):
+            rows = lhs[SLOTS * lo : SLOTS * hi]
+            groups = dot(rows, rhs).astype(BF).reshape(hi - lo, SLOTS, 128)
+            trip_out[t, lo:hi] = groups
+            for i in range(lo, min(hi, SELF)):
+                trip_copy(t, i, PEERS[i]).start()
+            if part == 1:
+                trip_in[t, SELF] = groups[SELF - lo]
+
+    def finish_trip(t, lhs):
+        trip_part(t, 1).wait_recv()
+        total = dot(lhs[:, SLOTS * FAR :], trip_in[t, FAR:].reshape(ROWS - SLOTS * FAR, 128))
+        trip_part(t, 0).wait_recv()
+        return total + dot(lhs[:, : SLOTS * FAR], trip_in[t, :FAR].reshape(SLOTS * FAR, 128))
 
     lane = iota((32, 128), 1)
     has = {
@@ -221,34 +307,46 @@
                 planes.append(v[l, r] - STEP * twice + NOISE_SCALE * noise)
         return planes
 
-    wanted = None
+    for l in range(2):
+        line_all(1, l).wait_recv()
+        line_all(0, l).wait_recv()
+        asked = ask_in[l].reshape(256, 128)
+        row_e, lane_e = (iota((256, 128), 0) // 2) % RING, iota((256, 128), 1) // 64
+        wide = jnp.concatenate(
+            [jnp.where(row_e == 2 * m + lane_e, asked, jnp.zeros_like(asked)) for m in range(RING // 2)], axis=1
+        )
+        answer = dot(wide, seed_in[l].reshape(512, 128)).astype(BF).reshape(2 * RING, LINE_ROWS, 128)
+        answer_out[l] = answer
+        answer_in[l, 0] = answer[0]
+        for q in ACROSS:
+            line_copy(answer_out.at[l, q], answer_in.at[l, q], 2, l, negative(across(l, q))).start()
+    start_trip(0, pick_t, cell)
+
     for k in range(STEPS):
-        x = x_buf[k].reshape(128, 128).astype(BF)
-        if k == 0:
-            trip_all(0).wait_recv()
-            wanted = trip_in[0].reshape(ROWS, 128)
-        send = dot(wanted, x).astype(BF).reshape(GROUPS, SLOTS, 128)
-        trip_out[1 + 2 * k] = send
-        trip_in[1 + 2 * k, SELF] = send[SELF]
-        start_trip(1 + 2 * k)
         if k > 0:
+            start_trip(2 * k, trip_in[0].reshape(ROWS, 128), x_buf[k].reshape(128, 128).astype(BF))
             start_halo(k)
         planes = prior(k)
-        trip_all(1 + 2 * k).wait_recv()
-        cells_in = dot(pick_ref[...], trip_in[1 + 2 * k].reshape(ROWS, 128)).astype(BF)
+        if k > 0:
+            cells_in = finish_trip(2 * k, pick_ref).astype(BF)
+        else:
+            halves = []
+            for l in range(2):
+                line_all(2, l).wait_recv()
+                halves.append(dot(pick_line_ref[l], answer_in[l].reshape(256, 128)))
+            cells_in = jnp.concatenate(halves, axis=0).astype(BF)
         parts = []
         for p in range(8):
             seen = dot(cells_in[16 * p : 16 * p + 16], weight_t_ref[p])
             misfit = gain_ref[16 * p : 16 * p + 16] * seen - offset_ref[16 * p : 16 * p + 16]
             w = weight_ref[p // 4, 16 * (p % 4) : 16 * (p % 4) + 16].reshape(256, 128)
             parts.append(dot(misfit.astype(BF), w).astype(BF))
-        adjoint = jnp.concatenate(parts, axis=0)
-        send = dot(pick_t_ref[...], adjoint).astype(BF).reshape(GROUPS, SLOTS, 128)
-        trip_out[2 + 2 * k] = send
-        trip_in[2 + 2 * k, SELF] = send[SELF]
-        start_trip(2 + 2 * k)
-        trip_all(2 + 2 * k).wait_recv()
-        total = dot(wanted, trip_in[2 + 2 * k].reshape(ROWS, 128), ((0,), (0,)))
+        start_trip(1 + 2 * k, pick_t_ref, jnp.concatenate(parts, axis=0))
+        if k == 0:
+            trip_part(0, 0).wait_recv()
+            trip_part(0, 1).wait_recv()
+            wanted_t_ref[...] = trip_in[0].reshape(ROWS, 128).T
+        total = finish_trip(1 + 2 * k, wanted_t_ref)
         for l in range(2):
             for r in range(2):
                 q = 2 * l + r
@@ -258,22 +356,32 @@
                 else:
                     out_ref[l, r : r + 1, :] = new.reshape(1, 4096)
 
-    for t in range(1 + 2 * STEPS):
-        trip_all(t).wait_send()
+    for what in range(3):
+        for l in range(2):
+            line_all(what, l).wait_send()
+    for t in range(2 * STEPS):
+        trip_part(t, 0).wait_send()
+        trip_part(t, 1).wait_send()
     for k in range(STEPS):
         halo_all(k).wait_send()
     kappa_all().wait_send()
 
 
-def per_device(slots, *arrays):
-    vmem = pl.BlockSpec(memory_space=pltpu.VMEM)
-    trips = 1 + 2 * STEPS
+def per_device(
+    slots, field, kappa_sq, noise, block_owner, block_cell, live_count, obs_weight, obs_value, obs_prec
+):
+    operands = (
+        slots, field, kappa_sq, noise, block_owner.transpose(0, 2, 1), block_cell, live_count.transpose(1, 0),
+        obs_weight, obs_value.transpose(0, 2, 1), obs_prec.transpose(0, 2, 1),
+    )
+    trips = 2 * STEPS
     return pl.pallas_call(
         kernel_body,
         out_shape=jax.ShapeDtypeStruct((2, 2, 4096), F32),
-        in_specs=[vmem] * 10,
-        out_specs=vmem,
+        in_specs=[pl.BlockSpec(memory_space=pltpu.HBM)] * 10,
+        out_specs=pl.BlockSpec(memory_space=pltpu.VMEM),
         scratch_shapes=[
+            *[pltpu.VMEM(a.shape, a.dtype) for a in operands],
             pltpu.VMEM((trips, GROUPS, SLOTS, 128), BF),
             pltpu.VMEM((trips, GROUPS, SLOTS, 128), BF),
             pltpu.VMEM((STEPS, 20, 32, 128), F32),
@@ -285,16 +393,24 @@
             pltpu.VMEM((128, 256), F32),
             pltpu.VMEM((128, 256), F32),
             pltpu.VMEM((8, 128, 256), BF),
-            pltpu.SemaphoreType.DMA((trips,)),
-            pltpu.SemaphoreType.DMA((trips,)),
+            pltpu.VMEM((128, ROWS), BF),
+            pltpu.VMEM((2, 64, 128), BF),
+            pltpu.VMEM((2, RING, 64, 128), BF),
+            *[pltpu.VMEM((2, 2 * RING, LINE_ROWS, 128), BF)] * 4,
+            pltpu.VMEM((2, 64, 256), BF),
+            pltpu.SemaphoreType.DMA((trips, 2)),
+            pltpu.SemaphoreType.DMA((trips, 2)),
             pltpu.SemaphoreType.DMA((STEPS + 1,)),
             pltpu.SemaphoreType.DMA((STEPS + 1,)),
+            pltpu.SemaphoreType.DMA((10,)),
+            pltpu.SemaphoreType.DMA((3, 2)),
+            pltpu.SemaphoreType.DMA((3, 2)),
         ],
         compiler_params=pltpu.CompilerParams(
-            collective_id=0, has_side_effects=True, vmem_limit_bytes=48 << 20
+            collective_id=0, has_side_effects=True, vmem_limit_bytes=60 << 20
         ),
         cost_estimate=pl.CostEstimate(flops=200_000_000, bytes_accessed=1_000_000, transcendentals=0),
-    )(slots, *arrays)
+    )(*operands)
 
 
 def slot_table():

time: 79.1 us -> 72.4 us (0.915)
  local copies, waits for them, and re-layouts: 5.87 us -> 1.47 us
  Pallas kernels: 72.8 us -> 70.8 us
    unnamed x19 -> x1, local copies, waits for them, and re-layouts: 5.87 us -> 1.47 us
    pallas_call x1, Pallas kernels: 72.8 us -> 70.8 us  [per_device(): pl.pallas_call(kernel_body, out_shape=jax.ShapeDtypeStruct((2, 2, 4096),...]
where the time goes in v2:
time: 72.4 us; the launch traced here: 72.3 us
  Pallas kernels  70.8 us (98%)
  local copies, waits for them, and re-layouts  1.47 us (2%)
    pallas_call x1, Pallas kernels, per_device(): pl.pallas_call(kernel_body, out_shape=jax.ShapeDtypeStruct((2, 2, 4096),...  70.8 us
    unnamed x1, local copies, waits for them, and re-layouts  1.47 us

profile of v2, /device:TPU:1, one launch (start us, length us, event | category | flops | bytes accessed | tf_op | source)
XLA Modules:
  0.0 72.3 jit_solution(17599448705009463558)
XLA Ops:
  0.0 70.8 %shard_map.100 = f32[2,2,4096]{2,1,0:T(2,128)} custom-call(s32[8,512]{1,0:T(8,128)} %constant.2.clone.slot_hbm, f32[2,2,4096]{2,1,0:T(2,128)} %field_hbm.1, f32[2,2,4096]{2,1,0:T(2,128)} %kappa_hbm.1, f32[3,2,2,4096]{3,2,1,0:T(2,128)} %noise_hbm.1, s32[2,1,64]{2,1,0:T(1,128)} %bitcast.8, s32[2,64]{1,0:T(2,128)} %cell_hbm.1, s32[1,2]{1,0:T(1,128)} %bitcast.9, ...), custom_call_target="tpu_custom_call" | custom-call | flops 200000000 | bytes 1000000 | tf_op jit(solution)/shard_map/pallas_call | solution.py:378
  70.8 1.5 %copy.13 = f32[2,2,4096]{2,1,0:T(2,128)} copy(f32[2,2,4096]{2,1,0:T(2,128)} %shard_map.100) | data formatting | bytes 131072

commit v3 on v2

--- a/solution.py
+++ b/solution.py
@@ -1,3 +1,5 @@
+import functools
+
 import jax
 import jax.numpy as jnp
 from jax import lax
@@ -64,7 +66,7 @@
     slot_hbm, field_hbm, kappa_hbm, noise_hbm, owner_hbm, cell_hbm, live_hbm, weight_hbm, value_hbm, prec_hbm,
     out_ref,
     slot_ref, field_ref, kappa_ref, noise_ref, owner_ref, cell_ref, live_ref, weight_ref, value_ref, prec_ref,
-    trip_out, trip_in, halo_x, halo_k, x_buf, k_buf, pick_ref, pick_t_ref, gain_ref, offset_ref, weight_t_ref,
+    trip_out, trip_in, near_x, far_x, halo_k, x_buf, k_buf, x_sent, k_sent, pick_ref, pick_t_ref, gain_ref, offset_ref, weight_t_ref,
     wanted_t_ref, seed_out, seed_in, ask_out, ask_in, answer_out, answer_in, pick_line_ref,
     trip_send, trip_recv, halo_send, halo_recv, load_sem, line_send, line_recv,
 ):
@@ -105,8 +107,10 @@
         load.wait()
     for l in range(2):
         for r in range(2):
-            x_buf[0, 2 * l + r] = field_ref[l, r : r + 1, :].reshape(32, 128)
-            k_buf[2 * l + r] = kappa_ref[l, r : r + 1, :].reshape(32, 128)
+            x_plane = field_ref[l, r : r + 1, :].reshape(32, 128)
+            k_plane = kappa_ref[l, r : r + 1, :].reshape(32, 128)
+            x_buf[0, 2 * l + r], x_sent[0, 2 * l + r] = x_plane, x_plane.astype(BF)
+            k_buf[2 * l + r], k_sent[2 * l + r] = k_plane, k_plane.astype(BF)
 
     owner_row = jnp.concatenate([owner_ref[0], owner_ref[1]], axis=1).astype(F32)
     owner = jnp.broadcast_to(owner_row, (128, 128)).T.astype(jnp.int32)[:, 0:1]
@@ -117,7 +121,7 @@
     rank = jnp.sum(dot(before, named.astype(BF)) * named, axis=1, keepdims=True).astype(jnp.int32)
     n = iota((1, 256), 1)
     for l in range(2):
-        x_flat = jnp.concatenate([x_buf[0, 2 * l], x_buf[0, 2 * l + 1]], axis=0).astype(BF)
+        x_flat = x_sent[0, 2 * l : 2 * l + 2].reshape(64, 128)
         seed_out[l] = x_flat
         seed_in[l, 0] = x_flat
         e, d = (n // 2) % RING, n // 32
@@ -146,45 +150,49 @@
         ref = seed_in.at[l, rest] if what == 0 else (ask_in if what == 1 else answer_in).at[l, others]
         return line_copy(ref, ref, what, l, (0, 0, 1))
 
+    for q in ACROSS:
+        for l in range(2):
+            line_copy(ask_out.at[l, q], ask_in.at[l, q], 1, l, across(l, q)).start()
     for e in OUTWARD:
         for l in range(2):
             line_copy(seed_out.at[l], seed_in.at[l, RING - e], 0, l, along(l, e)).start()
-    for q in ACROSS:
-        for l in range(2):
-            line_copy(ask_out.at[l, q], ask_in.at[l, q], 1, l, across(l, q)).start()
-
-    def halo_copy(src, dst, s, device):
+
+    def halo_copy(src, dst, kind, s, device):
         return pltpu.make_async_remote_copy(
-            src, dst, halo_send.at[s], halo_recv.at[s], device_id=device, device_id_type=MESH
+            src, dst, halo_send.at[kind, s], halo_recv.at[kind, s], device_id=device, device_id_type=MESH
         )
 
     def start_halo(k):
-        x = x_buf.at[k]
-        into = halo_x.at[k]
-        halo_copy(x, into.at[pl.ds(0, 4)], k, (me, above)).start()
-        halo_copy(x, into.at[pl.ds(4, 4)], k, (me, below)).start()
-        halo_copy(x, into.at[pl.ds(8, 4)], k, (north, lev)).start()
-        halo_copy(x, into.at[pl.ds(12, 4)], k, (south, lev)).start()
-        halo_copy(x.at[3], into.at[16], k, (north, above)).start()
-        halo_copy(x.at[2], into.at[17], k, (south, above)).start()
-        halo_copy(x.at[1], into.at[18], k, (north, below)).start()
-        halo_copy(x.at[0], into.at[19], k, (south, below)).start()
+        x, sent = x_buf.at[k], x_sent.at[k]
+        near, far = near_x.at[k], far_x.at[k]
+        halo_copy(x.at[pl.ds(2, 2)], near.at[pl.ds(0, 2)], 0, k, (me, above)).start()
+        halo_copy(x.at[pl.ds(0, 2)], near.at[pl.ds(2, 2)], 0, k, (me, below)).start()
+        halo_copy(sent.at[pl.ds(0, 2)], far.at[pl.ds(0, 2)], 1, k, (me, above)).start()
+        halo_copy(sent.at[pl.ds(2, 2)], far.at[pl.ds(2, 2)], 1, k, (me, below)).start()
+        for l in range(2):
+            halo_copy(x.at[2 * l + 1], near.at[4 + l], 0, k, (north, lev)).start()
+            halo_copy(x.at[2 * l], near.at[6 + l], 0, k, (south, lev)).start()
+            halo_copy(sent.at[2 * l], far.at[4 + l], 1, k, (north, lev)).start()
+            halo_copy(sent.at[2 * l + 1], far.at[6 + l], 1, k, (south, lev)).start()
+        halo_copy(sent.at[3], far.at[8], 1, k, (north, above)).start()
+        halo_copy(sent.at[2], far.at[9], 1, k, (south, above)).start()
+        halo_copy(sent.at[1], far.at[10], 1, k, (north, below)).start()
+        halo_copy(sent.at[0], far.at[11], 1, k, (south, below)).start()
 
     def halo_all(k):
-        return halo_copy(halo_x.at[k], halo_x.at[k], k, (north, lev))
+        return [
+            halo_copy(ref.at[k], ref.at[k], kind, k, (north, lev)) for kind, ref in enumerate((near_x, far_x))
+        ]
 
     def start_kappa():
-        halo_copy(k_buf.at[pl.ds(2, 2)], halo_k.at[pl.ds(0, 2)], STEPS, (me, above)).start()
-        halo_copy(k_buf.at[pl.ds(0, 2)], halo_k.at[pl.ds(2, 2)], STEPS, (me, below)).start()
-        for l in range(2):
-            halo_copy(k_buf.at[2 * l + 1], halo_k.at[4 + l], STEPS, (north, lev)).start()
-            halo_copy(k_buf.at[2 * l], halo_k.at[6 + l], STEPS, (south, lev)).start()
+        halo_copy(k_sent.at[pl.ds(2, 2)], halo_k.at[pl.ds(0, 2)], 1, STEPS, (me, above)).start()
+        halo_copy(k_sent.at[pl.ds(0, 2)], halo_k.at[pl.ds(2, 2)], 1, STEPS, (me, below)).start()
+        for l in range(2):
+            halo_copy(k_sent.at[2 * l + 1], halo_k.at[4 + l], 1, STEPS, (north, lev)).start()
+            halo_copy(k_sent.at[2 * l], halo_k.at[6 + l], 1, STEPS, (south, lev)).start()
 
     def kappa_all():
-        return halo_copy(halo_k, halo_k, STEPS, (north, lev))
-
-    start_halo(0)
-    start_kappa()
+        return halo_copy(halo_k, halo_k, 1, STEPS, (north, lev))
 
     slot_peer = slot_ref[0:1, :]
     slot_y, slot_z, slot_c = slot_ref[1:2, :], slot_ref[2:3, :], slot_ref[3:4, :]
@@ -240,8 +248,10 @@
             if part == 1:
                 trip_in[t, SELF] = groups[SELF - lo]
 
-    def finish_trip(t, lhs):
+    def finish_trip(t, lhs, meanwhile=None):
         trip_part(t, 1).wait_recv()
+        if meanwhile is not None:
+            meanwhile()
         total = dot(lhs[:, SLOTS * FAR :], trip_in[t, FAR:].reshape(ROWS - SLOTS * FAR, 128))
         trip_part(t, 0).wait_recv()
         return total + dot(lhs[:, : SLOTS * FAR], trip_in[t, :FAR].reshape(SLOTS * FAR, 128))
@@ -259,7 +269,8 @@
         return (kap + 6.0) * v - (near + left + right)
 
     def prior(k):
-        halo_all(k).wait_recv()
+        for copy in halo_all(k):
+            copy.wait_recv()
         if k == 0:
             kappa_all().wait_recv()
         v, kap = {}, {}
@@ -267,14 +278,13 @@
             for r in range(2):
                 v[l, r] = x_buf[k, 2 * l + r]
                 kap[l, r] = k_buf[2 * l + r]
-                v[l - 2, r] = halo_x[k, 2 * l + r]
-                v[l + 2, r] = halo_x[k, 4 + 2 * l + r]
-                v[l, r - 2] = halo_x[k, 8 + 2 * l + r]
-                v[l, r + 2] = halo_x[k, 12 + 2 * l + r]
-        v[-1, -1], v[-1, 2], v[2, -1], v[2, 2] = (halo_x[k, 16 + q] for q in range(4))
         for q in range(2):
-            kap[-1, q], kap[2, q] = halo_k[q], halo_k[2 + q]
-            kap[q, -1], kap[q, 2] = halo_k[4 + q], halo_k[6 + q]
+            v[-1, q], v[2, q], v[q, -1], v[q, 2] = (near_x[k, 2 * side + q] for side in range(4))
+            v[-2, q], v[3, q], v[q, -2], v[q, 3] = (far_x[k, 2 * side + q].astype(F32) for side in range(4))
+        v[-1, -1], v[-1, 2], v[2, -1], v[2, 2] = (far_x[k, 8 + q].astype(F32) for q in range(4))
+        for q in range(2):
+            kap[-1, q], kap[2, q] = halo_k[q].astype(F32), halo_k[2 + q].astype(F32)
+            kap[q, -1], kap[q, 2] = halo_k[4 + q].astype(F32), halo_k[6 + q].astype(F32)
 
         def inside(l, r):
             conds = []
@@ -320,28 +330,34 @@
         answer_in[l, 0] = answer[0]
         for q in ACROSS:
             line_copy(answer_out.at[l, q], answer_in.at[l, q], 2, l, negative(across(l, q))).start()
-    start_trip(0, pick_t, cell)
 
     for k in range(STEPS):
         if k > 0:
-            start_trip(2 * k, trip_in[0].reshape(ROWS, 128), x_buf[k].reshape(128, 128).astype(BF))
-            start_halo(k)
-        planes = prior(k)
+            start_trip(2 * k, trip_in[0].reshape(ROWS, 128), x_sent[k].reshape(128, 128))
+        else:
+            start_trip(0, pick_t, cell)
         if k > 0:
-            cells_in = finish_trip(2 * k, pick_ref).astype(BF)
+            cells_in = finish_trip(2 * k, pick_ref, functools.partial(start_halo, k)).astype(BF)
         else:
             halves = []
             for l in range(2):
                 line_all(2, l).wait_recv()
+                if l == 0:
+                    start_halo(0)
+                    start_kappa()
                 halves.append(dot(pick_line_ref[l], answer_in[l].reshape(256, 128)))
             cells_in = jnp.concatenate(halves, axis=0).astype(BF)
-        parts = []
+        misfits = []
         for p in range(8):
             seen = dot(cells_in[16 * p : 16 * p + 16], weight_t_ref[p])
             misfit = gain_ref[16 * p : 16 * p + 16] * seen - offset_ref[16 * p : 16 * p + 16]
+            misfits.append(misfit.astype(BF))
+        parts = []
+        for p in range(8):
             w = weight_ref[p // 4, 16 * (p % 4) : 16 * (p % 4) + 16].reshape(256, 128)
-            parts.append(dot(misfit.astype(BF), w).astype(BF))
+            parts.append(dot(misfits[p], w).astype(BF))
         start_trip(1 + 2 * k, pick_t_ref, jnp.concatenate(parts, axis=0))
+        planes = prior(k)
         if k == 0:
             trip_part(0, 0).wait_recv()
             trip_part(0, 1).wait_recv()
@@ -352,7 +368,7 @@
                 q = 2 * l + r
                 new = planes[q] - STEP * total[32 * q : 32 * q + 32]
                 if k + 1 < STEPS:
-                    x_buf[k + 1, q] = new
+                    x_buf[k + 1, q], x_sent[k + 1, q] = new, new.astype(BF)
                 else:
                     out_ref[l, r : r + 1, :] = new.reshape(1, 4096)
 
@@ -363,7 +379,8 @@
         trip_part(t, 0).wait_send()
         trip_part(t, 1).wait_send()
     for k in range(STEPS):
-        halo_all(k).wait_send()
+        for copy in halo_all(k):
+            copy.wait_send()
     kappa_all().wait_send()
 
 
@@ -384,10 +401,13 @@
             *[pltpu.VMEM(a.shape, a.dtype) for a in operands],
             pltpu.VMEM((trips, GROUPS, SLOTS, 128), BF),
             pltpu.VMEM((trips, GROUPS, SLOTS, 128), BF),
-            pltpu.VMEM((STEPS, 20, 32, 128), F32),
-            pltpu.VMEM((8, 32, 128), F32),
+            pltpu.VMEM((STEPS, 8, 32, 128), F32),
+            pltpu.VMEM((STEPS, 12, 32, 128), BF),
+            pltpu.VMEM((8, 32, 128), BF),
             pltpu.VMEM((STEPS, 4, 32, 128), F32),
             pltpu.VMEM((4, 32, 128), F32),
+            pltpu.VMEM((STEPS, 4, 32, 128), BF),
+            pltpu.VMEM((4, 32, 128), BF),
             pltpu.VMEM((128, ROWS), BF),
             pltpu.VMEM((ROWS, 128), BF),
             pltpu.VMEM((128, 256), F32),
@@ -400,17 +420,17 @@
             pltpu.VMEM((2, 64, 256), BF),
             pltpu.SemaphoreType.DMA((trips, 2)),
             pltpu.SemaphoreType.DMA((trips, 2)),
-            pltpu.SemaphoreType.DMA((STEPS + 1,)),
-            pltpu.SemaphoreType.DMA((STEPS + 1,)),
+            pltpu.SemaphoreType.DMA((2, STEPS + 1)),
+            pltpu.SemaphoreType.DMA((2, STEPS + 1)),
             pltpu.SemaphoreType.DMA((10,)),
             pltpu.SemaphoreType.DMA((3, 2)),
             pltpu.SemaphoreType.DMA((3, 2)),
         ],
         compiler_params=pltpu.CompilerParams(
-            collective_id=0, has_side_effects=True, vmem_limit_bytes=60 << 20
+            collective_id=0, has_side_effects=True, vmem_limit_bytes=40 << 20
         ),
         cost_estimate=pl.CostEstimate(flops=200_000_000, bytes_accessed=1_000_000, transcendentals=0),
-    )(*operands)
+    )(*[pltpu.with_memory_space_constraint(a, pltpu.HBM) for a in operands])
 
 
 def slot_table():

time: 72.4 us -> 68.1 us (0.941)
  Pallas kernels: 70.8 us -> 67.4 us
  local copies, waits for them, and re-layouts: 1.47 us -> 0.63 us
    pallas_call x1, Pallas kernels: 70.8 us -> 67.4 us  [per_device(): pl.pallas_call(kernel_body, out_shape=jax.ShapeDtypeStruct((2, 2, 4096),...]
    unnamed x1, local copies, waits for them, and re-layouts: 1.47 us -> 0.63 us
where the time goes in v3:
time: 68.1 us; the launch traced here: 68 us
  Pallas kernels  67.4 us (99%)
    pallas_call x1, Pallas kernels, per_device(): pl.pallas_call(kernel_body, out_shape=jax.ShapeDtypeStruct((2, 2, 4096),...  67.4 us

profile of v3, /device:TPU:1, one launch (start us, length us, event | category | flops | bytes accessed | tf_op | source)
XLA Modules:
  0.0 68.0 jit_solution(13976935776352157556)
XLA Ops:
  0.0 67.4 %shard_map.100 = f32[2,2,4096]{2,1,0:T(2,128)S(1)} custom-call(s32[8,512]{1,0:T(8,128)} %constant.2.clone.slot_hbm, f32[2,2,4096]{2,1,0:T(2,128)} %field_hbm.1, f32[2,2,4096]{2,1,0:T(2,128)} %kappa_hbm.1, f32[3,2,2,4096]{3,2,1,0:T(2,128)} %noise_hbm.1, s32[2,1,64]{2,1,0:T(1,128)} %bitcast.8, s32[2,64]{1,0:T(2,128)} %cell_hbm.1, s32[1,2]{1,0:T(1,128)} %bitcast.9, ...), custom_call_target="tpu_custom_call" | custom-call | flops 200000000 | bytes 1000000 | tf_op jit(solution)/shard_map/pallas_call | solution.py:395
  67.4 0.6 copy.13

commit v4 on v3

--- a/solution.py
+++ b/solution.py
@@ -26,13 +26,13 @@
 
 PEERS = sorted(
     [(a, b, c) for a in range(RING) for b in range(RING) for c in range(2) if (a, b, c) != (0, 0, 0)],
-    key=lambda d: (-hops(d), (d[0] + 3 * d[1]) % 4, d),
+    key=lambda d: (-hops(d), d[2], d[0], d[1]),
 )
 SELF = len(PEERS)
 GROUPS = SELF + 1
 SLOTS = 4
 ROWS = GROUPS * SLOTS
-FAR = 32
+FAR = 64
 
 OUTWARD = (4, 3, 5, 2, 6, 1, 7)
 LINE_ROWS = 2 * RING
@@ -317,15 +317,17 @@
                 planes.append(v[l, r] - STEP * twice + NOISE_SCALE * noise)
         return planes
 
+    wides = []
     for l in range(2):
         line_all(1, l).wait_recv()
-        line_all(0, l).wait_recv()
         asked = ask_in[l].reshape(256, 128)
         row_e, lane_e = (iota((256, 128), 0) // 2) % RING, iota((256, 128), 1) // 64
-        wide = jnp.concatenate(
+        wides.append(jnp.concatenate(
             [jnp.where(row_e == 2 * m + lane_e, asked, jnp.zeros_like(asked)) for m in range(RING // 2)], axis=1
-        )
-        answer = dot(wide, seed_in[l].reshape(512, 128)).astype(BF).reshape(2 * RING, LINE_ROWS, 128)
+        ))
+    for l in range(2):
+        line_all(0, l).wait_recv()
+        answer = dot(wides[l], seed_in[l].reshape(512, 128)).astype(BF).reshape(2 * RING, LINE_ROWS, 128)
         answer_out[l] = answer
         answer_in[l, 0] = answer[0]
         for q in ACROSS:

time: 68.1 us -> 67.3 us (0.988)
  Pallas kernels: 67.4 us -> 66.5 us
    pallas_call x1, Pallas kernels: 67.4 us -> 66.5 us  [per_device(): pl.pallas_call(kernel_body, out_shape=jax.ShapeDtypeStruct((2, 2, 4096),...]
where the time goes in v4:
time: 67.3 us; the launch traced here: 67.2 us
  Pallas kernels  66.5 us (99%)
    pallas_call x1, Pallas kernels, per_device(): pl.pallas_call(kernel_body, out_shape=jax.ShapeDtypeStruct((2, 2, 4096),...  66.5 us

profile of v4, /device:TPU:1, one launch (start us, length us, event | category | flops | bytes accessed | tf_op | source)
XLA Modules:
  0.0 67.2 jit_solution(9309113051598697708)
XLA Ops:
  0.0 66.5 %shard_map.100 = f32[2,2,4096]{2,1,0:T(2,128)S(1)} custom-call(s32[8,512]{1,0:T(8,128)} %constant.2.clone.slot_hbm, f32[2,2,4096]{2,1,0:T(2,128)} %field_hbm.1, f32[2,2,4096]{2,1,0:T(2,128)} %kappa_hbm.1, f32[3,2,2,4096]{3,2,1,0:T(2,128)} %noise_hbm.1, s32[2,1,64]{2,1,0:T(1,128)} %bitcast.8, s32[2,64]{1,0:T(2,128)} %cell_hbm.1, s32[1,2]{1,0:T(1,128)} %bitcast.9, ...), custom_call_target="tpu_custom_call" | custom-call | flops 200000000 | bytes 1000000 | tf_op jit(solution)/shard_map/pallas_call | solution.py:397
  66.5 0.6 copy.13
